TPU v7x, 32 devices: a whole 2x2x4 slice. The times are simulated.
32 devices in a mesh: rad: 8 (over y, x, core), azi: 4 (over z).
Axes of the slice: x: 2, y: 2, z: 4, core: 2. Of those that a mesh axis runs over, the one named last changes fastest.
Arguments:
- state: float32 [5, 4, 128, 512], P(None, None, 'rad', 'azi'), may hold values from -6 to 6
- shifts: int32 [128], replicated, may hold values from 0 to 511
- spin: float32 [128], replicated, may hold values from 0.2 to 1
- drift: float32 [128], replicated, may hold values from -1.5 to 1.5
- stiffness: float32 [4, 128], replicated, may hold values from 0.5 to 2
Outputs:
- evolved: float32 [5, 4, 128, 512], P(None, None, 'rad', 'azi')
All inputs are finite; a program needn't handle non-finite values.
Results may differ from a plain program's by a relative error of at most 0.00002.
Values sent between devices are 32-bit elements; how exact they have to be, the bound alone decides.
A program may use at most 64 MiB of HBM per device.

v0:
```python
import jax
import jax.numpy as jnp
from jax import lax
from jax.sharding import PartitionSpec as P

STEPS = 2


time_step = 0.15
diffuse = 0.05


def extended_2(block, sides, width, periodic):
    for axis, dim in sides:
        count = lax.axis_size(axis)
        forward = [(i, i + 1) for i in range(count - 1)]
        if periodic:
            forward.append((count - 1, 0))
        backward = [(target, source) for source, target in forward]
        low = lax.ppermute(
            lax.slice_in_dim(block, block.shape[dim] - width, None, axis=dim), axis, forward
        )
        high = lax.ppermute(lax.slice_in_dim(block, 0, width, axis=dim), axis, backward)
        block = jnp.concatenate([low, block, high], axis=dim)
    return block


def from_behind(block, axis, distance):
    devices = range(lax.axis_size(axis))
    route = [((i - distance) % len(devices), i) for i in devices]
    return lax.ppermute(block, axis, route)


def tendency(extended, stiff_rows, spin_rows, drift_rows):
    centre_cells = extended[:, :, 1:-1, 1:-1]
    upper_row = extended[:, :, 2:, 1:-1]
    lower_row = extended[:, :, :-2, 1:-1]
    ahead_cell = extended[:, :, 1:-1, 2:]
    behind_cell = extended[:, :, 1:-1, :-2]
    rad_slope = 0.5 * (upper_row - lower_row)
    azi_slope = 0.5 * (ahead_cell - behind_cell)
    laplace_sum = upper_row + lower_row + ahead_cell + behind_cell - 4.0 * centre_cells
    vertical_pad = jnp.pad(centre_cells[3:5], ((0, 0), (1, 1), (0, 0), (0, 0)))
    ver_slope = 0.5 * (vertical_pad[:, 2:] - vertical_pad[:, :-2])
    spin_col = spin_rows[:, None]
    drift_col = drift_rows[:, None]
    divergence = rad_slope[1] + azi_slope[2] + ver_slope[0]
    coupled = jnp.stack(
        [
            -divergence,
            2.0 * spin_col * centre_cells[2] - rad_slope[4],
            -0.5 * spin_col * centre_cells[1] - azi_slope[4],
            -ver_slope[1],
            -stiff_rows[:, :, None] * divergence,
        ]
    )
    return coupled - drift_col * azi_slope + diffuse * laplace_sum


def barrel_roll(block, amounts, length):
    result = block
    for bit_index in range((length - 1).bit_length()):
        taken = amounts // (1 << bit_index) % 2 == 1
        result = jnp.where(taken[None, :, None], jnp.roll(result, 1 << bit_index, axis=2), result)
    return result


def on_device(state, shifts, spin, drift, stiffness):
    planes, levels, rows, cells = state.shape
    rad_start = lax.axis_index("rad") * rows

    def rows_of(values, offset, count):
        padded = jnp.pad(values, [(0, 0)] * (values.ndim - 1) + [(3, 3)])
        return lax.dynamic_slice_in_dim(padded, rad_start + offset + 3, count, axis=values.ndim - 1)

    def coefs(offset, count):
        return (
            rows_of(stiffness, offset, count),
            rows_of(spin, offset, count),
            rows_of(drift, offset, count),
        )

    def operator(field):
        extended = extended_2(field, (("rad", 2),), 1, False)
        extended = extended_2(extended, (("azi", 3),), 1, True)
        return tendency(extended, *coefs(0, rows))

    local_shifts = rows_of(shifts, 0, rows)
    current = state
    for step_index in range(STEPS):
        first = current + time_step * operator(current)
        second = 0.75 * current + 0.25 * (first + time_step * operator(first))
        sectioned = current / 3.0 + 2.0 / 3.0 * (second + time_step * operator(second))
        flat = sectioned.reshape(planes * levels, rows, cells)
        tile_count = lax.axis_size("azi")
        hops = local_shifts // cells
        offsets = local_shifts % cells
        moved = flat
        for bit_index in range(tile_count.bit_length() - 1):
            arrived = from_behind(moved, "azi", 1 << bit_index)
            taken = hops // (1 << bit_index) % 2 == 1
            moved = jnp.where(taken[None, :, None], arrived, moved)
        before = from_behind(moved, "azi", 1)
        paired = jnp.concatenate([before, moved], axis=2)
        flat = barrel_roll(paired, offsets, cells)[:, :, cells:]
        current = flat.reshape(planes, levels, rows, cells)
    return current


def solution(mesh):
    in_specs = (P(None, None, "rad", "azi"), P(), P(), P(), P())
    out_specs = P(None, None, "rad", "azi")
    return jax.shard_map(
        on_device, mesh=mesh, in_specs=in_specs, out_specs=out_specs, check_vma=False
    )
```

profile of v0, /device:TPU:1, one launch (start us, length us, event | category | flops | bytes accessed | tf_op | source)
XLA Modules:
  0.0 189.8 jit_solution(4042959580250295229)
XLA Ops:
  0.9 4.5 %collective-permute-start.1 = (f32[5,4,1,128]{3,2,1,0:T(1,128)S(1)}, f32[5,4,1,128]{3,2,1,0:T(1,128)S(1)}, u32[]{:S(2)}, u32[]{:S(2)}) collective-permute-start(f32[5,4,1,128]{3,2,1,0:T(1,128)S(1)} %get-tuple-element.44), channel_id=1, source_target_pairs={{0,4},{4,8},{8,12},{12,16},{16,20},{20,24},{24,28},{1,5},{5,9},{9,... | collective-permute-start | bytes 30728 | tf_op jit(solution)/shard_map/ppermute | solution.py:20
  14.2 6.2 %collective-permute-done.3 = f32[5,4,18,1]{3,2,1,0:T(8,128)S(1)} collective-permute-done((f32[5,4,18,1]{3,2,1,0:T(8,128)S(1)}, f32[5,4,18,1]{3,2,1,0:T(8,128)S(1)}, u32[]{:S(2)}, u32[]{:S(2)}) %collective-permute-start.3) | collective-permute-done | bytes 1472 | tf_op jit(solution)/shard_map/ppermute | solution.py:20
  20.4 3.4 %collective-permute-done.2 = f32[5,4,18,1]{3,2,1,0:T(8,128)S(1)} collective-permute-done((f32[5,4,18,1]{3,2,1,0:T(8,128)S(1)}, f32[5,4,18,1]{3,2,1,0:T(8,128)S(1)}, u32[]{:S(2)}, u32[]{:S(2)}) %collective-permute-start.2) | collective-permute-done | bytes 1472 | tf_op jit(solution)/shard_map/ppermute | solution.py:23
  24.6 4.6 %collective-permute-start.5 = (f32[5,4,1,128]{3,2,1,0:T(1,128)S(1)}, f32[5,4,1,128]{3,2,1,0:T(1,128)S(1)}, u32[]{:S(2)}, u32[]{:S(2)}) collective-permute-start(f32[5,4,1,128]{3,2,1,0:T(1,128)S(1)} %get-tuple-element.42), channel_id=1, source_target_pairs={{0,4},{4,8},{8,12},{12,16},{16,20},{20,24},{24,28},{1,5},{5,9},{9,... | collective-permute-start | bytes 30728 | tf_op jit(solution)/shard_map/ppermute | solution.py:20
  31.3 2.9 %collective-permute-done.4 = f32[5,4,1,128]{3,2,1,0:T(1,128)S(1)} collective-permute-done((f32[5,4,1,128]{3,2,1,0:T(1,128)S(1)}, f32[5,4,1,128]{3,2,1,0:T(1,128)S(1)}, u32[]{:S(2)}, u32[]{:S(2)}) %collective-permute-start.4) | collective-permute-done | bytes 10272 | tf_op jit(solution)/shard_map/ppermute | solution.py:23
  35.2 2.5 %collective-permute-start.6 = (f32[5,4,18,1]{3,2,1,0:T(8,128)S(1)}, f32[5,4,18,1]{3,2,1,0:T(8,128)S(1)}, u32[]{:S(2)}, u32[]{:S(2)}) collective-permute-start(f32[5,4,18,1]{3,2,1,0:T(8,128)S(1)} %get-tuple-element.19), channel_id=1, source_target_pairs={{1,0},{2,1},{3,2},{0,3},{5,4},{6,5},{7,6},{4,7},{9,8},{10,9},{11,1... | collective-permute-start | bytes 4328 | tf_op jit(solution)/shard_map/ppermute | solution.py:23
  37.7 6.3 %collective-permute-done.7 = f32[5,4,18,1]{3,2,1,0:T(8,128)S(1)} collective-permute-done((f32[5,4,18,1]{3,2,1,0:T(8,128)S(1)}, f32[5,4,18,1]{3,2,1,0:T(8,128)S(1)}, u32[]{:S(2)}, u32[]{:S(2)}) %collective-permute-start.7) | collective-permute-done | bytes 1472 | tf_op jit(solution)/shard_map/ppermute | solution.py:20
  44.0 3.0 %collective-permute-done.6 = f32[5,4,18,1]{3,2,1,0:T(8,128)S(1)} collective-permute-done((f32[5,4,18,1]{3,2,1,0:T(8,128)S(1)}, f32[5,4,18,1]{3,2,1,0:T(8,128)S(1)}, u32[]{:S(2)}, u32[]{:S(2)}) %collective-permute-start.6) | collective-permute-done | bytes 1472 | tf_op jit(solution)/shard_map/ppermute | solution.py:23
  47.8 3.5 %collective-permute-start.9 = (f32[5,4,1,128]{3,2,1,0:T(1,128)S(1)}, f32[5,4,1,128]{3,2,1,0:T(1,128)S(1)}, u32[]{:S(2)}, u32[]{:S(2)}) collective-permute-start(f32[5,4,1,128]{3,2,1,0:T(1,128)S(1)} %get-tuple-element.40), channel_id=1, source_target_pairs={{0,4},{4,8},{8,12},{12,16},{16,20},{20,24},{24,28},{1,5},{5,9},{9,... | collective-permute-start | bytes 30728 | tf_op jit(solution)/shard_map/ppermute | solution.py:20
  53.4 2.9 %collective-permute-done.8 = f32[5,4,1,128]{3,2,1,0:T(1,128)S(1)} collective-permute-done((f32[5,4,1,128]{3,2,1,0:T(1,128)S(1)}, f32[5,4,1,128]{3,2,1,0:T(1,128)S(1)}, u32[]{:S(2)}, u32[]{:S(2)}) %collective-permute-start.8) | collective-permute-done | bytes 10272 | tf_op jit(solution)/shard_map/ppermute | solution.py:23
  56.6 3.2 %collective-permute-start.10 = (f32[5,4,18,1]{3,2,1,0:T(8,128)S(1)}, f32[5,4,18,1]{3,2,1,0:T(8,128)S(1)}, u32[]{:S(2)}, u32[]{:S(2)}) collective-permute-start(f32[5,4,18,1]{3,2,1,0:T(8,128)S(1)} %get-tuple-element.17), channel_id=1, source_target_pairs={{1,0},{2,1},{3,2},{0,3},{5,4},{6,5},{7,6},{4,7},{9,8},{10,9},{11,1... | collective-permute-start | bytes 4328 | tf_op jit(solution)/shard_map/ppermute | solution.py:23
  59.9 6.3 %collective-permute-done.11 = f32[5,4,18,1]{3,2,1,0:T(8,128)S(1)} collective-permute-done((f32[5,4,18,1]{3,2,1,0:T(8,128)S(1)}, f32[5,4,18,1]{3,2,1,0:T(8,128)S(1)}, u32[]{:S(2)}, u32[]{:S(2)}) %collective-permute-start.11) | collective-permute-done | bytes 1472 | tf_op jit(solution)/shard_map/ppermute | solution.py:20
  66.1 2.3 %collective-permute-done.10 = f32[5,4,18,1]{3,2,1,0:T(8,128)S(1)} collective-permute-done((f32[5,4,18,1]{3,2,1,0:T(8,128)S(1)}, f32[5,4,18,1]{3,2,1,0:T(8,128)S(1)}, u32[]{:S(2)}, u32[]{:S(2)}) %collective-permute-start.10) | collective-permute-done | bytes 1472 | tf_op jit(solution)/shard_map/ppermute | solution.py:23
  69.7 7.3 %collective-permute-done.12 = f32[20,16,128]{2,1,0:T(8,128)S(1)} collective-permute-done((f32[20,16,128]{2,1,0:T(8,128)S(1)}, f32[20,16,128]{2,1,0:T(8,128)S(1)}, u32[]{:S(2)}, u32[]{:S(2)}) %collective-permute-start.12) | collective-permute-done | bytes 163872 | tf_op jit(solution)/shard_map/ppermute | solution.py:31
  77.2 9.0 %collective-permute-done.13 = f32[20,16,128]{2,1,0:T(8,128)S(1)} collective-permute-done((f32[20,16,128]{2,1,0:T(8,128)S(1)}, f32[20,16,128]{2,1,0:T(8,128)S(1)}, u32[]{:S(2)}, u32[]{:S(2)}) %collective-permute-start.13) | collective-permute-done | bytes 163872 | tf_op jit(solution)/shard_map/ppermute | solution.py:31
  86.5 6.9 %collective-permute-done.14 = f32[20,16,128]{2,1,0:T(8,128)S(1)} collective-permute-done((f32[20,16,128]{2,1,0:T(8,128)S(1)}, f32[20,16,128]{2,1,0:T(8,128)S(1)}, u32[]{:S(2)}, u32[]{:S(2)}) %collective-permute-start.14) | collective-permute-done | bytes 163872 | tf_op jit(solution)/shard_map/ppermute | solution.py:31
  95.3 4.7 %collective-permute-start.16 = (f32[5,4,1,128]{3,2,1,0:T(1,128)S(1)}, f32[5,4,1,128]{3,2,1,0:T(1,128)S(1)}, u32[]{:S(2)}, u32[]{:S(2)}) collective-permute-start(f32[5,4,1,128]{3,2,1,0:T(1,128)S(1)} %get-tuple-element.38), channel_id=1, source_target_pairs={{0,4},{4,8},{8,12},{12,16},{16,20},{20,24},{24,28},{1,5},{5,9},{9,... | collective-permute-start | bytes 30728 | tf_op jit(solution)/shard_map/ppermute | solution.py:20
  101.9 3.0 %collective-permute-done.15 = f32[5,4,1,128]{3,2,1,0:T(1,128)S(1)} collective-permute-done((f32[5,4,1,128]{3,2,1,0:T(1,128)S(1)}, f32[5,4,1,128]{3,2,1,0:T(1,128)S(1)}, u32[]{:S(2)}, u32[]{:S(2)}) %collective-permute-start.15) | collective-permute-done | bytes 10272 | tf_op jit(solution)/shard_map/ppermute | solution.py:23
  105.2 3.3 %collective-permute-start.17 = (f32[5,4,18,1]{3,2,1,0:T(8,128)S(1)}, f32[5,4,18,1]{3,2,1,0:T(8,128)S(1)}, u32[]{:S(2)}, u32[]{:S(2)}) collective-permute-start(f32[5,4,18,1]{3,2,1,0:T(8,128)S(1)} %get-tuple-element.15), channel_id=1, source_target_pairs={{1,0},{2,1},{3,2},{0,3},{5,4},{6,5},{7,6},{4,7},{9,8},{10,9},{11,1... | collective-permute-start | bytes 4328 | tf_op jit(solution)/shard_map/ppermute | solution.py:23
  108.5 6.3 %collective-permute-done.18 = f32[5,4,18,1]{3,2,1,0:T(8,128)S(1)} collective-permute-done((f32[5,4,18,1]{3,2,1,0:T(8,128)S(1)}, f32[5,4,18,1]{3,2,1,0:T(8,128)S(1)}, u32[]{:S(2)}, u32[]{:S(2)}) %collective-permute-start.18) | collective-permute-done | bytes 1472 | tf_op jit(solution)/shard_map/ppermute | solution.py:20
  117.6 4.3 %collective-permute-start.20 = (f32[5,4,1,128]{3,2,1,0:T(1,128)S(1)}, f32[5,4,1,128]{3,2,1,0:T(1,128)S(1)}, u32[]{:S(2)}, u32[]{:S(2)}) collective-permute-start(f32[5,4,1,128]{3,2,1,0:T(1,128)S(1)} %get-tuple-element.36), channel_id=1, source_target_pairs={{0,4},{4,8},{8,12},{12,16},{16,20},{20,24},{24,28},{1,5},{5,9},{9,... | collective-permute-start | bytes 30728 | tf_op jit(solution)/shard_map/ppermute | solution.py:20
  123.8 3.1 %collective-permute-done.19 = f32[5,4,1,128]{3,2,1,0:T(1,128)S(1)} collective-permute-done((f32[5,4,1,128]{3,2,1,0:T(1,128)S(1)}, f32[5,4,1,128]{3,2,1,0:T(1,128)S(1)}, u32[]{:S(2)}, u32[]{:S(2)}) %collective-permute-start.19) | collective-permute-done | bytes 10272 | tf_op jit(solution)/shard_map/ppermute | solution.py:23
  127.1 3.3 %collective-permute-start.21 = (f32[5,4,18,1]{3,2,1,0:T(8,128)S(1)}, f32[5,4,18,1]{3,2,1,0:T(8,128)S(1)}, u32[]{:S(2)}, u32[]{:S(2)}) collective-permute-start(f32[5,4,18,1]{3,2,1,0:T(8,128)S(1)} %get-tuple-element.13), channel_id=1, source_target_pairs={{1,0},{2,1},{3,2},{0,3},{5,4},{6,5},{7,6},{4,7},{9,8},{10,9},{11,1... | collective-permute-start | bytes 4328 | tf_op jit(solution)/shard_map/ppermute | solution.py:23
  130.4 6.3 %collective-permute-done.22 = f32[5,4,18,1]{3,2,1,0:T(8,128)S(1)} collective-permute-done((f32[5,4,18,1]{3,2,1,0:T(8,128)S(1)}, f32[5,4,18,1]{3,2,1,0:T(8,128)S(1)}, u32[]{:S(2)}, u32[]{:S(2)}) %collective-permute-start.22) | collective-permute-done | bytes 1472 | tf_op jit(solution)/shard_map/ppermute | solution.py:20
  136.7 2.8 %collective-permute-done.21 = f32[5,4,18,1]{3,2,1,0:T(8,128)S(1)} collective-permute-done((f32[5,4,18,1]{3,2,1,0:T(8,128)S(1)}, f32[5,4,18,1]{3,2,1,0:T(8,128)S(1)}, u32[]{:S(2)}, u32[]{:S(2)}) %collective-permute-start.21) | collective-permute-done | bytes 1472 | tf_op jit(solution)/shard_map/ppermute | solution.py:23
  140.3 4.5 %collective-permute-start.24 = (f32[5,4,1,128]{3,2,1,0:T(1,128)S(1)}, f32[5,4,1,128]{3,2,1,0:T(1,128)S(1)}, u32[]{:S(2)}, u32[]{:S(2)}) collective-permute-start(f32[5,4,1,128]{3,2,1,0:T(1,128)S(1)} %get-tuple-element.34), channel_id=1, source_target_pairs={{0,4},{4,8},{8,12},{12,16},{16,20},{20,24},{24,28},{1,5},{5,9},{9,... | collective-permute-start | bytes 30728 | tf_op jit(solution)/shard_map/ppermute | solution.py:20
  146.8 3.1 %collective-permute-done.23 = f32[5,4,1,128]{3,2,1,0:T(1,128)S(1)} collective-permute-done((f32[5,4,1,128]{3,2,1,0:T(1,128)S(1)}, f32[5,4,1,128]{3,2,1,0:T(1,128)S(1)}, u32[]{:S(2)}, u32[]{:S(2)}) %collective-permute-start.23) | collective-permute-done | bytes 10272 | tf_op jit(solution)/shard_map/ppermute | solution.py:23
  153.4 6.3 %collective-permute-done.26 = f32[5,4,18,1]{3,2,1,0:T(8,128)S(1)} collective-permute-done((f32[5,4,18,1]{3,2,1,0:T(8,128)S(1)}, f32[5,4,18,1]{3,2,1,0:T(8,128)S(1)}, u32[]{:S(2)}, u32[]{:S(2)}) %collective-permute-start.26) | collective-permute-done | bytes 1472 | tf_op jit(solution)/shard_map/ppermute | solution.py:20
  159.6 3.5 %collective-permute-done.25 = f32[5,4,18,1]{3,2,1,0:T(8,128)S(1)} collective-permute-done((f32[5,4,18,1]{3,2,1,0:T(8,128)S(1)}, f32[5,4,18,1]{3,2,1,0:T(8,128)S(1)}, u32[]{:S(2)}, u32[]{:S(2)}) %collective-permute-start.25) | collective-permute-done | bytes 1472 | tf_op jit(solution)/shard_map/ppermute | solution.py:23
  164.2 7.1 %collective-permute-done.27 = f32[20,16,128]{2,1,0:T(8,128)S(1)} collective-permute-done((f32[20,16,128]{2,1,0:T(8,128)S(1)}, f32[20,16,128]{2,1,0:T(8,128)S(1)}, u32[]{:S(2)}, u32[]{:S(2)}) %collective-permute-start.27) | collective-permute-done | bytes 163872 | tf_op jit(solution)/shard_map/ppermute | solution.py:31
  171.5 8.7 %collective-permute-done.28 = f32[20,16,128]{2,1,0:T(8,128)S(1)} collective-permute-done((f32[20,16,128]{2,1,0:T(8,128)S(1)}, f32[20,16,128]{2,1,0:T(8,128)S(1)}, u32[]{:S(2)}, u32[]{:S(2)}) %collective-permute-start.28) | collective-permute-done | bytes 163872 | tf_op jit(solution)/shard_map/ppermute | solution.py:31
  180.4 7.0 %collective-permute-done.29 = f32[20,16,128]{2,1,0:T(8,128)S(1)} collective-permute-done((f32[20,16,128]{2,1,0:T(8,128)S(1)}, f32[20,16,128]{2,1,0:T(8,128)S(1)}, u32[]{:S(2)}, u32[]{:S(2)}) %collective-permute-start.29) | collective-permute-done | bytes 163872 | tf_op jit(solution)/shard_map/ppermute | solution.py:31
  (172 shorter events, 37.0 us)
Async XLA Ops:
  0.9 8.1 %collective-permute-start.1 = (f32[5,4,1,128]{3,2,1,0:T(1,128)S(1)}, f32[5,4,1,128]{3,2,1,0:T(1,128)S(1)}, u32[]{:S(2)}, u32[]{:S(2)}) collective-permute-start(f32[5,4,1,128]{3,2,1,0:T(1,128)S(1)} %get-tuple-element.44), channel_id=1, source_target_pairs={{0,4},{4,8},{8,12},{12,16},{16,20},{20,24},{24,28},{1,5},{5,9},{9,... | collective-permute-start | bytes 30728 | tf_op jit(solution)/shard_map/ppermute | solution.py:20
  5.5 5.0 %collective-permute-start = (f32[5,4,1,128]{3,2,1,0:T(1,128)S(1)}, f32[5,4,1,128]{3,2,1,0:T(1,128)S(1)}, u32[]{:S(2)}, u32[]{:S(2)}) collective-permute-start(f32[5,4,1,128]{3,2,1,0:T(1,128)S(1)} %get-tuple-element.45), channel_id=1, source_target_pairs={{4,0},{8,4},{12,8},{16,12},{20,16},{24,20},{28,24},{5,1},{9,5},{13... | collective-permute-start | bytes 30728 | tf_op jit(solution)/shard_map/ppermute | solution.py:23
  10.7 9.7 %collective-permute-start.3 = (f32[5,4,18,1]{3,2,1,0:T(8,128)S(1)}, f32[5,4,18,1]{3,2,1,0:T(8,128)S(1)}, u32[]{:S(2)}, u32[]{:S(2)}) collective-permute-start(f32[5,4,18,1]{3,2,1,0:T(8,128)S(1)} %get-tuple-element.20), channel_id=1, source_target_pairs={{0,1},{1,2},{2,3},{3,0},{4,5},{5,6},{6,7},{7,4},{8,9},{9,10},{10,1... | collective-permute-start | bytes 4328 | tf_op jit(solution)/shard_map/ppermute | solution.py:20
  12.0 11.8 %collective-permute-start.2 = (f32[5,4,18,1]{3,2,1,0:T(8,128)S(1)}, f32[5,4,18,1]{3,2,1,0:T(8,128)S(1)}, u32[]{:S(2)}, u32[]{:S(2)}) collective-permute-start(f32[5,4,18,1]{3,2,1,0:T(8,128)S(1)} %get-tuple-element.21), channel_id=1, source_target_pairs={{1,0},{2,1},{3,2},{0,3},{5,4},{6,5},{7,6},{4,7},{9,8},{10,9},{11,1... | collective-permute-start | bytes 4328 | tf_op jit(solution)/shard_map/ppermute | solution.py:23
  24.6 6.7 %collective-permute-start.5 = (f32[5,4,1,128]{3,2,1,0:T(1,128)S(1)}, f32[5,4,1,128]{3,2,1,0:T(1,128)S(1)}, u32[]{:S(2)}, u32[]{:S(2)}) collective-permute-start(f32[5,4,1,128]{3,2,1,0:T(1,128)S(1)} %get-tuple-element.42), channel_id=1, source_target_pairs={{0,4},{4,8},{8,12},{12,16},{16,20},{20,24},{24,28},{1,5},{5,9},{9,... | collective-permute-start | bytes 30728 | tf_op jit(solution)/shard_map/ppermute | solution.py:20
  29.2 5.0 %collective-permute-start.4 = (f32[5,4,1,128]{3,2,1,0:T(1,128)S(1)}, f32[5,4,1,128]{3,2,1,0:T(1,128)S(1)}, u32[]{:S(2)}, u32[]{:S(2)}) collective-permute-start(f32[5,4,1,128]{3,2,1,0:T(1,128)S(1)} %get-tuple-element.43), channel_id=1, source_target_pairs={{4,0},{8,4},{12,8},{16,12},{20,16},{24,20},{28,24},{5,1},{9,5},{13... | collective-permute-start | bytes 30728 | tf_op jit(solution)/shard_map/ppermute | solution.py:23
  34.3 12.7 %copy-start.2 = (f32[5,4,16,128]{3,2,1,0:T(8,128)S(1)}, f32[5,4,16,128]{3,2,1,0:T(8,128)}, u32[]{:S(2)}) copy-start(f32[5,4,16,128]{3,2,1,0:T(8,128)} %copy-done.1) | copy-start | bytes 491524
  34.4 9.6 %collective-permute-start.7 = (f32[5,4,18,1]{3,2,1,0:T(8,128)S(1)}, f32[5,4,18,1]{3,2,1,0:T(8,128)S(1)}, u32[]{:S(2)}, u32[]{:S(2)}) collective-permute-start(f32[5,4,18,1]{3,2,1,0:T(8,128)S(1)} %get-tuple-element.18), channel_id=1, source_target_pairs={{0,1},{1,2},{2,3},{3,0},{4,5},{5,6},{6,7},{7,4},{8,9},{9,10},{10,1... | collective-permute-start | bytes 4328 | tf_op jit(solution)/shard_map/ppermute | solution.py:20
  35.2 11.8 %collective-permute-start.6 = (f32[5,4,18,1]{3,2,1,0:T(8,128)S(1)}, f32[5,4,18,1]{3,2,1,0:T(8,128)S(1)}, u32[]{:S(2)}, u32[]{:S(2)}) collective-permute-start(f32[5,4,18,1]{3,2,1,0:T(8,128)S(1)} %get-tuple-element.19), channel_id=1, source_target_pairs={{1,0},{2,1},{3,2},{0,3},{5,4},{6,5},{7,6},{4,7},{9,8},{10,9},{11,1... | collective-permute-start | bytes 4328 | tf_op jit(solution)/shard_map/ppermute | solution.py:23
  47.8 5.6 %collective-permute-start.9 = (f32[5,4,1,128]{3,2,1,0:T(1,128)S(1)}, f32[5,4,1,128]{3,2,1,0:T(1,128)S(1)}, u32[]{:S(2)}, u32[]{:S(2)}) collective-permute-start(f32[5,4,1,128]{3,2,1,0:T(1,128)S(1)} %get-tuple-element.40), channel_id=1, source_target_pairs={{0,4},{4,8},{8,12},{12,16},{16,20},{20,24},{24,28},{1,5},{5,9},{9,... | collective-permute-start | bytes 30728 | tf_op jit(solution)/shard_map/ppermute | solution.py:20
  51.3 5.0 %collective-permute-start.8 = (f32[5,4,1,128]{3,2,1,0:T(1,128)S(1)}, f32[5,4,1,128]{3,2,1,0:T(1,128)S(1)}, u32[]{:S(2)}, u32[]{:S(2)}) collective-permute-start(f32[5,4,1,128]{3,2,1,0:T(1,128)S(1)} %get-tuple-element.41), channel_id=1, source_target_pairs={{4,0},{8,4},{12,8},{16,12},{20,16},{24,20},{28,24},{5,1},{9,5},{13... | collective-permute-start | bytes 30728 | tf_op jit(solution)/shard_map/ppermute | solution.py:23
  56.5 9.6 %collective-permute-start.11 = (f32[5,4,18,1]{3,2,1,0:T(8,128)S(1)}, f32[5,4,18,1]{3,2,1,0:T(8,128)S(1)}, u32[]{:S(2)}, u32[]{:S(2)}) collective-permute-start(f32[5,4,18,1]{3,2,1,0:T(8,128)S(1)} %get-tuple-element.16), channel_id=1, source_target_pairs={{0,1},{1,2},{2,3},{3,0},{4,5},{5,6},{6,7},{7,4},{8,9},{9,10},{10,1... | collective-permute-start | bytes 4328 | tf_op jit(solution)/shard_map/ppermute | solution.py:20
  56.6 11.8 %collective-permute-start.10 = (f32[5,4,18,1]{3,2,1,0:T(8,128)S(1)}, f32[5,4,18,1]{3,2,1,0:T(8,128)S(1)}, u32[]{:S(2)}, u32[]{:S(2)}) collective-permute-start(f32[5,4,18,1]{3,2,1,0:T(8,128)S(1)} %get-tuple-element.17), channel_id=1, source_target_pairs={{1,0},{2,1},{3,2},{0,3},{5,4},{6,5},{7,6},{4,7},{9,8},{10,9},{11,1... | collective-permute-start | bytes 4328 | tf_op jit(solution)/shard_map/ppermute | solution.py:23
  69.2 7.9 %collective-permute-start.12 = (f32[20,16,128]{2,1,0:T(8,128)S(1)}, f32[20,16,128]{2,1,0:T(8,128)S(1)}, u32[]{:S(2)}, u32[]{:S(2)}) collective-permute-start(f32[20,16,128]{2,1,0:T(8,128)S(1)} %bitcast.46), channel_id=1, source_target_pairs={{3,0},{0,1},{1,2},{2,3},{7,4},{4,5},{5,6},{6,7},{11,8},{8,9},{9,10... | collective-permute-start | bytes 491528 | tf_op jit(solution)/shard_map/ppermute | solution.py:31
  77.1 9.1 %collective-permute-start.13 = (f32[20,16,128]{2,1,0:T(8,128)S(1)}, f32[20,16,128]{2,1,0:T(8,128)S(1)}, u32[]{:S(2)}, u32[]{:S(2)}) collective-permute-start(f32[20,16,128]{2,1,0:T(8,128)S(1)} %broadcast_select_fusion.1), channel_id=1, source_target_pairs={{2,0},{3,1},{0,2},{1,3},{6,4},{7,5},{4,6},{5,7},{10,8},{11,9},{8,1... | collective-permute-start | bytes 491528 | tf_op jit(solution)/shard_map/ppermute | solution.py:31
  86.3 7.1 %collective-permute-start.14 = (f32[20,16,128]{2,1,0:T(8,128)S(1)}, f32[20,16,128]{2,1,0:T(8,128)S(1)}, u32[]{:S(2)}, u32[]{:S(2)}) collective-permute-start(f32[20,16,128]{2,1,0:T(8,128)S(1)} %broadcast_select_fusion.3), channel_id=1, source_target_pairs={{3,0},{0,1},{1,2},{2,3},{7,4},{4,5},{5,6},{6,7},{11,8},{8,9},{9,10... | collective-permute-start | bytes 491528 | tf_op jit(solution)/shard_map/ppermute | solution.py:31
  95.3 6.6 %collective-permute-start.16 = (f32[5,4,1,128]{3,2,1,0:T(1,128)S(1)}, f32[5,4,1,128]{3,2,1,0:T(1,128)S(1)}, u32[]{:S(2)}, u32[]{:S(2)}) collective-permute-start(f32[5,4,1,128]{3,2,1,0:T(1,128)S(1)} %get-tuple-element.38), channel_id=1, source_target_pairs={{0,4},{4,8},{8,12},{12,16},{16,20},{20,24},{24,28},{1,5},{5,9},{9,... | collective-permute-start | bytes 30728 | tf_op jit(solution)/shard_map/ppermute | solution.py:20
  100.0 5.0 %collective-permute-start.15 = (f32[5,4,1,128]{3,2,1,0:T(1,128)S(1)}, f32[5,4,1,128]{3,2,1,0:T(1,128)S(1)}, u32[]{:S(2)}, u32[]{:S(2)}) collective-permute-start(f32[5,4,1,128]{3,2,1,0:T(1,128)S(1)} %get-tuple-element.39), channel_id=1, source_target_pairs={{4,0},{8,4},{12,8},{16,12},{20,16},{24,20},{28,24},{5,1},{9,5},{13... | collective-permute-start | bytes 30728 | tf_op jit(solution)/shard_map/ppermute | solution.py:23
  105.2 9.6 %collective-permute-start.18 = (f32[5,4,18,1]{3,2,1,0:T(8,128)S(1)}, f32[5,4,18,1]{3,2,1,0:T(8,128)S(1)}, u32[]{:S(2)}, u32[]{:S(2)}) collective-permute-start(f32[5,4,18,1]{3,2,1,0:T(8,128)S(1)} %get-tuple-element.14), channel_id=1, source_target_pairs={{0,1},{1,2},{2,3},{3,0},{4,5},{5,6},{6,7},{7,4},{8,9},{9,10},{10,1... | collective-permute-start | bytes 4328 | tf_op jit(solution)/shard_map/ppermute | solution.py:20
  105.2 11.5 %collective-permute-start.17 = (f32[5,4,18,1]{3,2,1,0:T(8,128)S(1)}, f32[5,4,18,1]{3,2,1,0:T(8,128)S(1)}, u32[]{:S(2)}, u32[]{:S(2)}) collective-permute-start(f32[5,4,18,1]{3,2,1,0:T(8,128)S(1)} %get-tuple-element.15), channel_id=1, source_target_pairs={{1,0},{2,1},{3,2},{0,3},{5,4},{6,5},{7,6},{4,7},{9,8},{10,9},{11,1... | collective-permute-start | bytes 4328 | tf_op jit(solution)/shard_map/ppermute | solution.py:23
  117.6 6.2 %collective-permute-start.20 = (f32[5,4,1,128]{3,2,1,0:T(1,128)S(1)}, f32[5,4,1,128]{3,2,1,0:T(1,128)S(1)}, u32[]{:S(2)}, u32[]{:S(2)}) collective-permute-start(f32[5,4,1,128]{3,2,1,0:T(1,128)S(1)} %get-tuple-element.36), channel_id=1, source_target_pairs={{0,4},{4,8},{8,12},{12,16},{16,20},{20,24},{24,28},{1,5},{5,9},{9,... | collective-permute-start | bytes 30728 | tf_op jit(solution)/shard_map/ppermute | solution.py:20
  121.9 5.0 %collective-permute-start.19 = (f32[5,4,1,128]{3,2,1,0:T(1,128)S(1)}, f32[5,4,1,128]{3,2,1,0:T(1,128)S(1)}, u32[]{:S(2)}, u32[]{:S(2)}) collective-permute-start(f32[5,4,1,128]{3,2,1,0:T(1,128)S(1)} %get-tuple-element.37), channel_id=1, source_target_pairs={{4,0},{8,4},{12,8},{16,12},{20,16},{24,20},{28,24},{5,1},{9,5},{13... | collective-permute-start | bytes 30728 | tf_op jit(solution)/shard_map/ppermute | solution.py:23
  127.1 9.6 %collective-permute-start.22 = (f32[5,4,18,1]{3,2,1,0:T(8,128)S(1)}, f32[5,4,18,1]{3,2,1,0:T(8,128)S(1)}, u32[]{:S(2)}, u32[]{:S(2)}) collective-permute-start(f32[5,4,18,1]{3,2,1,0:T(8,128)S(1)} %get-tuple-element.12), channel_id=1, source_target_pairs={{0,1},{1,2},{2,3},{3,0},{4,5},{5,6},{6,7},{7,4},{8,9},{9,10},{10,1... | collective-permute-start | bytes 4328 | tf_op jit(solution)/shard_map/ppermute | solution.py:20
  127.1 12.4 %collective-permute-start.21 = (f32[5,4,18,1]{3,2,1,0:T(8,128)S(1)}, f32[5,4,18,1]{3,2,1,0:T(8,128)S(1)}, u32[]{:S(2)}, u32[]{:S(2)}) collective-permute-start(f32[5,4,18,1]{3,2,1,0:T(8,128)S(1)} %get-tuple-element.13), channel_id=1, source_target_pairs={{1,0},{2,1},{3,2},{0,3},{5,4},{6,5},{7,6},{4,7},{9,8},{10,9},{11,1... | collective-permute-start | bytes 4328 | tf_op jit(solution)/shard_map/ppermute | solution.py:23
  140.3 6.5 %collective-permute-start.24 = (f32[5,4,1,128]{3,2,1,0:T(1,128)S(1)}, f32[5,4,1,128]{3,2,1,0:T(1,128)S(1)}, u32[]{:S(2)}, u32[]{:S(2)}) collective-permute-start(f32[5,4,1,128]{3,2,1,0:T(1,128)S(1)} %get-tuple-element.34), channel_id=1, source_target_pairs={{0,4},{4,8},{8,12},{12,16},{16,20},{20,24},{24,28},{1,5},{5,9},{9,... | collective-permute-start | bytes 30728 | tf_op jit(solution)/shard_map/ppermute | solution.py:20
  144.8 5.0 %collective-permute-start.23 = (f32[5,4,1,128]{3,2,1,0:T(1,128)S(1)}, f32[5,4,1,128]{3,2,1,0:T(1,128)S(1)}, u32[]{:S(2)}, u32[]{:S(2)}) collective-permute-start(f32[5,4,1,128]{3,2,1,0:T(1,128)S(1)} %get-tuple-element.35), channel_id=1, source_target_pairs={{4,0},{8,4},{12,8},{16,12},{20,16},{24,20},{28,24},{5,1},{9,5},{13... | collective-permute-start | bytes 30728 | tf_op jit(solution)/shard_map/ppermute | solution.py:23
  149.9 13.2 %copy-start.8 = (f32[5,4,16,128]{3,2,1,0:T(8,128)S(1)}, f32[5,4,16,128]{3,2,1,0:T(8,128)}, u32[]{:S(2)}) copy-start(f32[5,4,16,128]{3,2,1,0:T(8,128)} %copy-done.7) | copy-start | bytes 491524
  150.0 9.6 %collective-permute-start.26 = (f32[5,4,18,1]{3,2,1,0:T(8,128)S(1)}, f32[5,4,18,1]{3,2,1,0:T(8,128)S(1)}, u32[]{:S(2)}, u32[]{:S(2)}) collective-permute-start(f32[5,4,18,1]{3,2,1,0:T(8,128)S(1)} %get-tuple-element.10), channel_id=1, source_target_pairs={{0,1},{1,2},{2,3},{3,0},{4,5},{5,6},{6,7},{7,4},{8,9},{9,10},{10,1... | collective-permute-start | bytes 4328 | tf_op jit(solution)/shard_map/ppermute | solution.py:20
  151.3 11.8 %collective-permute-start.25 = (f32[5,4,18,1]{3,2,1,0:T(8,128)S(1)}, f32[5,4,18,1]{3,2,1,0:T(8,128)S(1)}, u32[]{:S(2)}, u32[]{:S(2)}) collective-permute-start(f32[5,4,18,1]{3,2,1,0:T(8,128)S(1)} %get-tuple-element.11), channel_id=1, source_target_pairs={{1,0},{2,1},{3,2},{0,3},{5,4},{6,5},{7,6},{4,7},{9,8},{10,9},{11,1... | collective-permute-start | bytes 4328 | tf_op jit(solution)/shard_map/ppermute | solution.py:23
  163.9 7.4 %collective-permute-start.27 = (f32[20,16,128]{2,1,0:T(8,128)S(1)}, f32[20,16,128]{2,1,0:T(8,128)S(1)}, u32[]{:S(2)}, u32[]{:S(2)}) collective-permute-start(f32[20,16,128]{2,1,0:T(8,128)S(1)} %bitcast.45), channel_id=1, source_target_pairs={{3,0},{0,1},{1,2},{2,3},{7,4},{4,5},{5,6},{6,7},{11,8},{8,9},{9,10... | collective-permute-start | bytes 491528 | tf_op jit(solution)/shard_map/ppermute | solution.py:31
  171.4 8.7 %collective-permute-start.28 = (f32[20,16,128]{2,1,0:T(8,128)S(1)}, f32[20,16,128]{2,1,0:T(8,128)S(1)}, u32[]{:S(2)}, u32[]{:S(2)}) collective-permute-start(f32[20,16,128]{2,1,0:T(8,128)S(1)} %broadcast_select_fusion), channel_id=1, source_target_pairs={{2,0},{3,1},{0,2},{1,3},{6,4},{7,5},{4,6},{5,7},{10,8},{11,9},{8,1... | collective-permute-start | bytes 491528 | tf_op jit(solution)/shard_map/ppermute | solution.py:31
  180.2 7.1 %collective-permute-start.29 = (f32[20,16,128]{2,1,0:T(8,128)S(1)}, f32[20,16,128]{2,1,0:T(8,128)S(1)}, u32[]{:S(2)}, u32[]{:S(2)}) collective-permute-start(f32[20,16,128]{2,1,0:T(8,128)S(1)} %broadcast_select_fusion.2), channel_id=1, source_target_pairs={{3,0},{0,1},{1,2},{2,3},{7,4},{4,5},{5,6},{6,7},{11,8},{8,9},{9,10... | collective-permute-start | bytes 491528 | tf_op jit(solution)/shard_map/ppermute | solution.py:31
  (16 other events, 93.6 us)
where the time goes:
time: 192 us; the launch traced here: 190 us
  waiting for transfers between devices  117 us (61%)
  starting transfers between devices  58.8 us (31%)
  other arithmetic  8.41 us (4%)
  local copies, waits for them, and re-layouts  4.76 us (2%)
    ppermute x6, waiting for transfers between devices, from_behind(): return lax.ppermute(block, axis, route)  46 us
    ppermute x12, waiting for transfers between devices, extended_2(): lax.ppermute(lax.slice_in_dim(block, block.shape[dim] - width, None, axis...  37.6 us
    ppermute x12, waiting for transfers between devices, extended_2(): lax.ppermute(lax.slice_in_dim(block, 0, width, axis=dim), axis, backward)  33.4 us
    ppermute x12, starting transfers between devices, extended_2(): lax.ppermute(lax.slice_in_dim(block, block.shape[dim] - width, None, axis...  29.8 us
    ppermute x12, starting transfers between devices, extended_2(): lax.ppermute(lax.slice_in_dim(block, 0, width, axis=dim), axis, backward)  27.9 us
  transfers between devices with their start and end apart: 30, of which 24 were waited for; matrix products, arithmetic and copies ran while one was open for 0% of the time, Pallas kernels for 0%

commit v1 on v0

v1 whole, which is shorter than its diff:
```python
import functools

import jax
import jax.numpy as jnp
from jax import lax
from jax.experimental import pallas as pl
from jax.experimental.pallas import tpu as pltpu
from jax.sharding import PartitionSpec as P

MESH = pl.DeviceIdType.MESH
STEPS = 2
HALO = 8
LANES = 128
LEVELS = 4
time_step = 0.15
diffuse = 0.05


def gather_kernel(nrad, nazi, x_ref, ext_ref, zeros, own_sem, z_send, z_recv, h_send, h_recv, edge_sem):
    rad, azi = lax.axis_index("rad"), lax.axis_index("azi")
    rows = x_ref.shape[1]
    has_low, has_high = rad > 0, rad < nrad - 1

    barrier = pltpu.get_barrier_semaphore()
    for d in range(1, nazi):
        pl.semaphore_signal(barrier, inc=1, device_id=(rad, lax.rem(azi + d, nazi)), device_id_type=MESH)

    @pl.when(has_low)
    def _():
        pl.semaphore_signal(barrier, inc=1, device_id=(rad - 1, azi), device_id_type=MESH)

    @pl.when(has_high)
    def _():
        pl.semaphore_signal(barrier, inc=1, device_id=(rad + 1, azi), device_id_type=MESH)

    own = pltpu.make_async_copy(x_ref, ext_ref.at[azi, :, pl.ds(HALO, rows)], own_sem)
    own.start()
    zeros[...] = jnp.zeros_like(zeros)
    pl.semaphore_wait(barrier, nazi - 1 + has_low.astype(jnp.int32) + has_high.astype(jnp.int32))

    def along(d):
        return pltpu.make_async_remote_copy(
            src_ref=x_ref,
            dst_ref=ext_ref.at[azi, :, pl.ds(HALO, rows)],
            send_sem=z_send.at[d],
            recv_sem=z_recv.at[d],
            device_id=(rad, lax.rem(azi + d, nazi)),
            device_id_type=MESH,
        )

    def to_low(d):
        block = lax.rem(azi + nazi - d, nazi)
        src = x_ref.at[:, pl.ds(0, HALO)] if d == 0 else ext_ref.at[block, :, pl.ds(HALO, HALO)]
        return pltpu.make_async_remote_copy(
            src_ref=src,
            dst_ref=ext_ref.at[block, :, pl.ds(HALO + rows, HALO)],
            send_sem=h_send.at[0, d],
            recv_sem=h_recv.at[0, d],
            device_id=(rad - 1, azi),
            device_id_type=MESH,
        )

    def to_high(d):
        block = lax.rem(azi + nazi - d, nazi)
        src = x_ref.at[:, pl.ds(rows - HALO, HALO)] if d == 0 else ext_ref.at[block, :, pl.ds(rows, HALO)]
        return pltpu.make_async_remote_copy(
            src_ref=src,
            dst_ref=ext_ref.at[block, :, pl.ds(0, HALO)],
            send_sem=h_send.at[1, d],
            recv_sem=h_recv.at[1, d],
            device_id=(rad + 1, azi),
            device_id_type=MESH,
        )

    def edge(b, side):
        start = 0 if side == 0 else HALO + rows
        return pltpu.make_async_copy(zeros, ext_ref.at[b, :, pl.ds(start, HALO)], edge_sem.at[side, b])

    order = sorted(range(1, nazi), key=lambda d: min(d, nazi - d))
    for d in order:
        along(d).start()
    for d in [0] + order:
        if d:
            along(d).wait_recv()

        @pl.when(has_low)
        def _():
            to_low(d).start()

        @pl.when(has_high)
        def _():
            to_high(d).start()

    @pl.when(jnp.logical_not(has_low))
    def _():
        for b in range(nazi):
            edge(b, 0).start()
        for b in range(nazi):
            edge(b, 0).wait()

    @pl.when(jnp.logical_not(has_high))
    def _():
        for b in range(nazi):
            edge(b, 1).start()
        for b in range(nazi):
            edge(b, 1).wait()

    own.wait()
    for d in order:
        along(d).wait_send()

    @pl.when(has_low)
    def _():
        for d in range(nazi):
            to_low(d).wait_send()
            to_high(d).wait_recv()

    @pl.when(has_high)
    def _():
        for d in range(nazi):
            to_high(d).wait_send()
            to_low(d).wait_recv()


def gathered(x, nrad, nazi):
    planes, rows, cells = x.shape
    return pl.pallas_call(
        functools.partial(gather_kernel, nrad, nazi),
        out_shape=jax.ShapeDtypeStruct((nazi, planes, rows + 2 * HALO, cells), jnp.float32),
        in_specs=[pl.BlockSpec(memory_space=pl.ANY)],
        out_specs=pl.BlockSpec(memory_space=pl.ANY),
        scratch_shapes=[
            pltpu.VMEM((planes, HALO, cells), jnp.float32),
            pltpu.SemaphoreType.DMA,
            pltpu.SemaphoreType.DMA((nazi,)),
            pltpu.SemaphoreType.DMA((nazi,)),
            pltpu.SemaphoreType.DMA((2, nazi)),
            pltpu.SemaphoreType.DMA((2, nazi)),
            pltpu.SemaphoreType.DMA((2, nazi)),
        ],
        compiler_params=pltpu.CompilerParams(collective_id=0, has_side_effects=True),
    )(x)


def starts_for(first, last):
    starts = list(range(first, last - 6, 8))
    if starts[-1] + 7 < last:
        starts.append(last - 7)
    return starts


def stage(src, base, dst, coef, first, last, old, new):
    nazi = src.shape[0]
    lane = lax.broadcasted_iota(jnp.int32, (8, LANES), 1)
    at_end, at_start = lane == LANES - 1, lane == 0

    def body(j, carry):
        before = lax.rem(j + nazi - 1, nazi)
        after = lax.rem(j + 1, nazi)
        for s in starts_for(first, last):
            c0, d, ga, gb, h, s2, s5 = (coef[i, s : s + 8, :] for i in range(7))
            stiff = [coef[7 + k, s : s + 8, :] for k in range(LEVELS)]

            def cell(f, k):
                return src[j, f * LEVELS + k, s : s + 8, :]

            def around(f, k):
                p = f * LEVELS + k
                c = src[j, p, s : s + 8, :]
                up, lo = src[j, p, s + 1 : s + 9, :], src[j, p, s - 1 : s + 7, :]
                be = pltpu.roll(jnp.where(at_end, src[before, p, s : s + 8, :], c), 1, 1)
                ah = pltpu.roll(jnp.where(at_start, src[after, p, s : s + 8, :], c), LANES - 1, 1)
                return c, up, lo, ah, be

            def rest(parts):
                c, up, lo, ah, be = parts
                return c0 * c + d * (up + lo) + (ga * ah + gb * be)

            def vertical(f, k):
                if k == 0:
                    return cell(f, 1)
                if k == LEVELS - 1:
                    return -cell(f, k - 1)
                return cell(f, k + 1) - cell(f, k - 1)

            for k in range(LEVELS):
                rho, u, v, w, p = (around(f, k) for f in range(5))
                div = (u[1] - u[2]) + (v[3] - v[4]) + vertical(3, k)
                results = (
                    rest(rho) - h * div,
                    rest(u) + s2 * v[0] - h * (p[1] - p[2]),
                    rest(v) - s5 * u[0] - h * (p[3] - p[4]),
                    rest(w) - h * vertical(4, k),
                    rest(p) - stiff[k] * div,
                )
                for f, result in enumerate(results):
                    plane = f * LEVELS + k
                    if base is not None:
                        result = old * base[j, plane, s : s + 8, :] + new * result
                    dst[j, plane, s : s + 8, :] = result
        return carry

    lax.fori_loop(0, nazi, body, 0)


def compute_kernel(azi_ref, ext_ref, coef_ref, out_ref, one, two, three):
    nazi, planes, rows, cells = ext_ref.shape
    reach = HALO
    low, high = HALO, rows - HALO - 1
    lane = lax.broadcasted_iota(jnp.int32, (8, LANES), 1)

    def section(current, margin, x, y, z):
        stage(current, None, x, coef_ref, low - margin - 2, high + margin + 2, 0.0, 1.0)
        stage(x, current, y, coef_ref, low - margin - 1, high + margin + 1, 0.75, 0.25)
        stage(y, current, z, coef_ref, low - margin, high + margin, 1.0 / 3.0, 2.0 / 3.0)

    def amounts(s):
        shift = coef_ref[11, s : s + 8, :].astype(jnp.int32)
        return shift // LANES, shift % LANES

    def rotate(here, behind, offsets):
        mixed = jnp.where(lane >= LANES - offsets, behind, here)
        return jnp.take_along_axis(mixed, lax.rem(lane - offsets + LANES, LANES), axis=1)

    section(ext_ref, 3, one, two, three)
    for s in starts_for(low - 3, high + 3):
        hops, offsets = amounts(s)

        def shifted(p, carry):
            blocks = [three[b, p, s : s + 8, :] for b in range(nazi)]
            blocks = [rotate(blocks[b], blocks[b - 1], offsets) for b in range(nazi)]
            for bit in range(nazi.bit_length() - 1):
                taken = (hops // (1 << bit)) % 2 == 1
                blocks = [jnp.where(taken, blocks[b - (1 << bit)], blocks[b]) for b in range(nazi)]
            for b in range(nazi):
                one[b, p, s : s + 8, :] = blocks[b]
            return carry

        lax.fori_loop(0, planes, shifted, 0)

    stage(one, None, two, coef_ref, low - 2, high + 2, 0.0, 1.0)
    stage(two, one, three, coef_ref, low - 1, high + 1, 0.75, 0.25)
    stage(three, one, two, coef_ref, low, high, 1.0 / 3.0, 2.0 / 3.0)
    azi = azi_ref[0]
    for s in starts_for(low, high):
        hops, offsets = amounts(s)
        source = lax.rem(azi - hops + nazi, nazi)

        def final(p, carry):
            blocks = [two[b, p, s : s + 8, :] for b in range(nazi)]
            here, behind = blocks[0], blocks[-1]
            for b in range(1, nazi):
                here = jnp.where(source == b, blocks[b], here)
                behind = jnp.where(source == b, blocks[b - 1], behind)
            out_ref[p, s - HALO : s, :] = rotate(here, behind, offsets)
            return carry

        lax.fori_loop(0, planes, final, 0)


def on_device(state, shifts, spin, drift, stiffness):
    fields, levels, rows, cells = state.shape
    planes = fields * levels
    nrad, nazi = lax.axis_size("rad"), lax.axis_size("azi")
    wide = rows + 2 * HALO
    flat = state.reshape(planes, rows, cells)

    c = time_step * diffuse
    half = 0.5 * time_step
    unit = jnp.ones_like(spin)
    table = jnp.concatenate(
        [
            jnp.stack(
                [
                    (1.0 - 4.0 * c) * unit,
                    c * unit,
                    c - half * drift,
                    c + half * drift,
                    half * unit,
                    2.0 * time_step * spin,
                    half * spin,
                ]
            ),
            half * stiffness,
            shifts.astype(jnp.float32)[None],
        ]
    )
    padded = jnp.pad(table, ((0, 0), (HALO, HALO)))
    mine = lax.dynamic_slice_in_dim(padded, lax.axis_index("rad") * rows, wide, axis=1)
    coef = jnp.broadcast_to(mine[:, :, None], (table.shape[0], wide, cells))
    place = lax.axis_index("azi").astype(jnp.int32).reshape(1)

    ext = gathered(flat, nrad, nazi)
    whole = pltpu.VMEM(ext.shape, jnp.float32)
    out = pl.pallas_call(
        compute_kernel,
        out_shape=jax.ShapeDtypeStruct(flat.shape, jnp.float32),
        in_specs=[
            pl.BlockSpec(memory_space=pltpu.SMEM),
            pl.BlockSpec(memory_space=pltpu.VMEM),
            pl.BlockSpec(memory_space=pltpu.VMEM),
        ],
        out_specs=pl.BlockSpec(memory_space=pltpu.VMEM),
        scratch_shapes=[whole, whole, whole],
        compiler_params=pltpu.CompilerParams(vmem_limit_bytes=40 * 2**20),
    )(place, ext, coef)
    return out.reshape(state.shape)


def solution(mesh):
    in_specs = (P(None, None, "rad", "azi"), P(), P(), P(), P())
    out_specs = P(None, None, "rad", "azi")
    return jax.shard_map(
        on_device, mesh=mesh, in_specs=in_specs, out_specs=out_specs, check_vma=False
    )
```

time: 192 us -> 42.7 us (0.22); the launches traced: 190 us -> 42.5 us
  waiting for transfers between devices: 117 us -> 0 us
  starting transfers between devices: 58.8 us -> 0 us
  Pallas kernels: 0 us -> 38.8 us
  other arithmetic: 8.41 us -> 2.01 us
  local copies, waits for them, and re-layouts: 4.76 us -> 1.63 us
    ppermute x30 -> x0, waiting for transfers between devices: 117 us -> none  [the longest x6 46 us: from_behind(): return lax.ppermute(block, axis, route)]
    ppermute x30 -> x0, starting transfers between devices: 58.8 us -> none  [the longest x12 29.8 us: extended_2(): lax.ppermute(lax.slice_in_dim(block, block.shape[dim] - width, None, axis...]
    pallas_call x0 -> x2, Pallas kernels: none -> 38.8 us  [the longest x1 24.8 us: gathered(): pl.pallas_call(functools.partial(gather_kernel, nrad, nazi), out_shape=ja...]
    slice x38 -> x0, local copies, waits for them, and re-layouts: 4.01 us -> none  [the longest x12 1.76 us: extended_2(): lax.slice_in_dim(block, block.shape[dim] - width, None, axis=dim)]
    select_n x18 -> x0, other arithmetic: 3.17 us -> none  [the longest x14 2.84 us: barrel_roll(): jnp.where(taken[None, :, None], jnp.roll(result, 1 << bit_index, axis=2),...]
  transfers between devices with their start and end apart: 30 -> 0, of which waited for: 24 -> 0; matrix products, arithmetic and copies ran while one was open for 0% -> 0% of each run, Pallas kernels for 0% -> 0%
where the time goes in v1:
time: 42.7 us; the launch traced here: 42.5 us
  Pallas kernels  38.8 us (91%)
  other arithmetic  2.01 us (5%)
  local copies, waits for them, and re-layouts  1.63 us (4%)
    pallas_call x1, Pallas kernels, gathered(): pl.pallas_call(functools.partial(gather_kernel, nrad, nazi), out_shape=ja...  24.8 us
    pallas_call x1, Pallas kernels, on_device(): pl.pallas_call(compute_kernel, out_shape=jax.ShapeDtypeStruct(flat.shape,...  14 us
    unnamed x2, local copies, waits for them, and re-layouts  1.31 us

profile of v1, /device:TPU:1, one launch (start us, length us, event | category | flops | bytes accessed | tf_op | source)
XLA Modules:
  0.0 42.5 jit_solution(15875451676920887346)
XLA Ops:
  0.0 0.7 %convert_bitcast_fusion = f32[1,128]{1,0:T(1,128)S(1)} fusion(s32[128]{0:T(128)} %param.6), kind=kLoop, calls=%fused_computation.2 | loop fusion | flops 128 | bytes 1024 | tf_op jit(solution)/shard_map/broadcast_in_dim | solution.py:285
  0.7 0.7 %broadcast_multiply_fusion = f32[4,128]{1,0:T(4,128)S(1)} fusion(f32[4,128]{1,0:T(4,128)} %param.9), kind=kLoop, calls=%fused_computation.1 | loop fusion | flops 512 | bytes 4096 | tf_op jit(solution)/shard_map/mul | solution.py:284
  1.3 0.7 %multiply_bitcast_fusion = (f32[1,128]{1,0:T(1,128)S(1)}, f32[1,128]{1,0:T(1,128)S(1)}, f32[1,128]{1,0:T(1,128)S(1)}, f32[1,128]{1,0:T(1,128)S(1)}) fusion(f32[128]{0:T(128)} %param.7, f32[128]{0:T(128)} %param.8), kind=kLoop, calls=%fused_computation.3 | loop fusion | flops 640 | bytes 3072 | tf_op jit(solution)/shard_map/stack | solution.py:273
  2.0 0.1 concatenate.3
  2.2 0.1 pad_dynamic-slice_fusion
  2.2 0.1 broadcast_in_dim.10.coef_ref
  2.3 24.8 %shard_map.55.ext_ref = f32[4,20,32,128]{3,2,1,0:T(8,128)} custom-call(f32[20,16,128]{2,1,0:T(8,128)} %bitcast.13), custom_call_target="tpu_custom_call" | custom-call | tf_op jit(solution)/shard_map/pallas_call | solution.py:127
  27.2 0.0 copy-start
  27.2 1.3 %copy-done = f32[4,20,32,128]{3,2,1,0:T(8,128)S(1)} copy-done((f32[4,20,32,128]{3,2,1,0:T(8,128)S(1)}, f32[4,20,32,128]{3,2,1,0:T(8,128)}, u32[]{:S(2)}) %copy-start) | copy-done | bytes 1310744
  28.5 14.0 %shard_map.56 = f32[20,16,128]{2,1,0:T(8,128)} custom-call(s32[1]{0:T(128)} %bitcast.azi_ref, f32[4,20,32,128]{3,2,1,0:T(8,128)S(1)} %copy-done, f32[12,32,128]{2,1,0:T(8,128)S(1)} %broadcast_in_dim.10.coef_ref), custom_call_target="tpu_custom_call" | custom-call | tf_op jit(solution)/shard_map/pallas_call | solution.py:295
  (3 shorter events, 0.0 us)
Async XLA Ops:
  27.2 1.3 %copy-start = (f32[4,20,32,128]{3,2,1,0:T(8,128)S(1)}, f32[4,20,32,128]{3,2,1,0:T(8,128)}, u32[]{:S(2)}) copy-start(f32[4,20,32,128]{3,2,1,0:T(8,128)} %shard_map.55.ext_ref) | copy-start | bytes 3932164

commit v2 on v1

v2 whole, which is shorter than its diff:
```python
import functools

import jax
import jax.numpy as jnp
from jax import lax
from jax.experimental import pallas as pl
from jax.experimental.pallas import tpu as pltpu
from jax.sharding import PartitionSpec as P

MESH = pl.DeviceIdType.MESH
STEPS = 2
HALO = 8
OWN = 16
LANES = 128
LEVELS = 4
time_step = 0.15
diffuse = 0.05


def gather_kernel(nrad, nazi, x_ref, ext_ref, zeros, own_sem, z_send, z_recv, h_send, h_recv, edge_sem):
    rad, azi = lax.axis_index("rad"), lax.axis_index("azi")
    rows = x_ref.shape[1]
    has_low, has_high = rad > 0, rad < nrad - 1

    has_left, has_right = azi > 0, azi < nazi - 1
    neighbours = ((has_left, rad, azi - 1), (has_right, rad, azi + 1), (has_low, rad - 1, azi), (has_high, rad + 1, azi))

    barrier = pltpu.get_barrier_semaphore()
    expected = 0
    for present, to_rad, to_azi in neighbours:
        expected = expected + present.astype(jnp.int32)

        @pl.when(present)
        def _():
            pl.semaphore_signal(barrier, inc=1, device_id=(to_rad, to_azi), device_id_type=MESH)

    own = pltpu.make_async_copy(x_ref, ext_ref.at[azi, :, pl.ds(OWN, rows)], own_sem)
    own.start()
    zeros[...] = jnp.zeros_like(zeros)
    pl.semaphore_wait(barrier, expected)

    def along(side, t):
        block = azi - t if side == 0 else azi + t
        src = x_ref if t == 0 else ext_ref.at[block, :, pl.ds(OWN, rows)]
        return pltpu.make_async_remote_copy(
            src_ref=src,
            dst_ref=ext_ref.at[block, :, pl.ds(OWN, rows)],
            send_sem=z_send.at[side, t],
            recv_sem=z_recv.at[side, t],
            device_id=(rad, azi + 1 if side == 0 else azi - 1),
            device_id_type=MESH,
        )

    def sends(side, t):
        if side == 0:
            return jnp.logical_and(azi - t >= 0, has_right)
        return jnp.logical_and(azi + t < nazi, has_left)

    def arrives(side, t):
        return azi - 1 - t >= 0 if side == 0 else azi + 1 + t < nazi

    def arrived(side, t):
        block = azi - 1 - t if side == 0 else azi + 1 + t
        return pltpu.make_async_remote_copy(
            src_ref=x_ref,
            dst_ref=ext_ref.at[block, :, pl.ds(OWN, rows)],
            send_sem=z_send.at[side, t],
            recv_sem=z_recv.at[side, t],
            device_id=(rad, azi + 1 if side == 0 else azi - 1),
            device_id_type=MESH,
        )

    def radial(to, block, own_block):
        if to == 0:
            start, there = 0, OWN + rows
        else:
            start, there = rows - HALO, OWN - HALO
        src = x_ref.at[:, pl.ds(start, HALO)] if own_block else ext_ref.at[block, :, pl.ds(OWN + start, HALO)]
        return pltpu.make_async_remote_copy(
            src_ref=src,
            dst_ref=ext_ref.at[block, :, pl.ds(there, HALO)],
            send_sem=h_send.at[to, block],
            recv_sem=h_recv.at[to, block],
            device_id=(rad - 1 if to == 0 else rad + 1, azi),
            device_id_type=MESH,
        )

    def pass_on(block, own_block=False):
        @pl.when(has_low)
        def _():
            radial(0, block, own_block).start()

        @pl.when(has_high)
        def _():
            radial(1, block, own_block).start()

    def edge(b, side):
        start = OWN - HALO if side == 0 else OWN + rows
        return pltpu.make_async_copy(zeros, ext_ref.at[b, :, pl.ds(start, HALO)], edge_sem.at[side, b])

    for side in range(2):

        @pl.when(sends(side, 0))
        def _():
            along(side, 0).start()

    pass_on(azi, True)
    for side, missing in enumerate((has_low, has_high)):

        @pl.when(jnp.logical_not(missing))
        def _():
            for b in range(nazi):
                edge(b, side).start()

    for t in range(nazi - 1):
        for side in range(2):

            @pl.when(arrives(side, t))
            def _():
                arrived(side, t).wait_recv()

                @pl.when(sends(side, t + 1))
                def _():
                    along(side, t + 1).start()

                pass_on(azi - 1 - t if side == 0 else azi + 1 + t)

    for side, missing in enumerate((has_low, has_high)):

        @pl.when(jnp.logical_not(missing))
        def _():
            for b in range(nazi):
                edge(b, side).wait()

    own.wait()
    for t in range(nazi - 1):
        for side in range(2):

            @pl.when(sends(side, t))
            def _():
                along(side, t).wait_send()

    @pl.when(has_low)
    def _():
        for b in range(nazi):
            radial(0, b, False).wait_send()
            radial(1, b, False).wait_recv()

    @pl.when(has_high)
    def _():
        for b in range(nazi):
            radial(1, b, False).wait_send()
            radial(0, b, False).wait_recv()


def gathered(x, nrad, nazi):
    planes, rows, cells = x.shape
    return pl.pallas_call(
        functools.partial(gather_kernel, nrad, nazi),
        out_shape=jax.ShapeDtypeStruct((nazi, planes, rows + 2 * OWN, cells), jnp.float32),
        in_specs=[pl.BlockSpec(memory_space=pl.ANY)],
        out_specs=pl.BlockSpec(memory_space=pl.ANY),
        scratch_shapes=[
            pltpu.VMEM((planes, HALO, cells), jnp.float32),
            pltpu.SemaphoreType.DMA,
            pltpu.SemaphoreType.DMA((2, nazi)),
            pltpu.SemaphoreType.DMA((2, nazi)),
            pltpu.SemaphoreType.DMA((2, nazi)),
            pltpu.SemaphoreType.DMA((2, nazi)),
            pltpu.SemaphoreType.DMA((2, nazi)),
        ],
        compiler_params=pltpu.CompilerParams(collective_id=0, has_side_effects=True),
    )(x)


def stage(src, base, dst, coef, tiles, old, new):
    nazi = src.shape[0]
    lane = lax.broadcasted_iota(jnp.int32, (8, LANES), 1)
    at_end, at_start = lane == LANES - 1, lane == 0

    def body(j, carry):
        before = lax.rem(j + nazi - 1, nazi)
        after = lax.rem(j + 1, nazi)
        for s in tiles:
            c0, d, ga, gb, h, s2, s5 = (coef[i, s : s + 8, :] for i in range(7))
            stiff = [coef[7 + k, s : s + 8, :] for k in range(LEVELS)]

            def cell(f, k):
                return src[j, f * LEVELS + k, s : s + 8, :]

            def around(f, k):
                p = f * LEVELS + k
                c = src[j, p, s : s + 8, :]
                up, lo = src[j, p, s + 1 : s + 9, :], src[j, p, s - 1 : s + 7, :]
                be = pltpu.roll(jnp.where(at_end, src[before, p, s : s + 8, :], c), 1, 1)
                ah = pltpu.roll(jnp.where(at_start, src[after, p, s : s + 8, :], c), LANES - 1, 1)
                return c, up, lo, ah, be

            def rest(parts):
                c, up, lo, ah, be = parts
                return c0 * c + d * (up + lo) + (ga * ah + gb * be)

            def vertical(f, k):
                if k == 0:
                    return cell(f, 1)
                if k == LEVELS - 1:
                    return -cell(f, k - 1)
                return cell(f, k + 1) - cell(f, k - 1)

            for k in range(LEVELS):
                rho, u, v, w, p = (around(f, k) for f in range(5))
                div = (u[1] - u[2]) + (v[3] - v[4]) + vertical(3, k)
                results = (
                    rest(rho) - h * div,
                    rest(u) + s2 * v[0] - h * (p[1] - p[2]),
                    rest(v) - s5 * u[0] - h * (p[3] - p[4]),
                    rest(w) - h * vertical(4, k),
                    rest(p) - stiff[k] * div,
                )
                for f, result in enumerate(results):
                    plane = f * LEVELS + k
                    if base is not None:
                        result = old * base[j, plane, s : s + 8, :] + new * result
                    dst[j, plane, s : s + 8, :] = result
        return carry

    lax.fori_loop(0, nazi, body, 0)


def fill_coefficients(coef, first, shift_ref, spin_ref, drift_ref, stiff_ref):
    count = coef.shape[1] - 2 * HALO
    shape = (count, spin_ref.shape[1])
    radius = lax.broadcasted_iota(jnp.int32, shape, 0) + first
    match = radius == lax.broadcasted_iota(jnp.int32, shape, 1)

    def column(values):
        picked = jnp.sum(jnp.where(match, values, 0.0), axis=1, keepdims=True)
        return jnp.broadcast_to(picked, (count, LANES))

    c = time_step * diffuse
    half = 0.5 * time_step
    inside = column(jnp.ones((1, shape[1]), jnp.float32))
    spin, drift = column(spin_ref[...]), column(drift_ref[...])
    values = [
        (1.0 - 4.0 * c) * inside,
        c * inside,
        c * inside - half * drift,
        c * inside + half * drift,
        half * inside,
        2.0 * time_step * spin,
        half * spin,
    ]
    values += [half * column(stiff_ref[k : k + 1, :]) for k in range(LEVELS)]
    values.append(column(shift_ref[...].astype(jnp.float32)))
    for i, value in enumerate(values):
        coef[i, HALO : HALO + count, :] = value


def compute_kernel(shift_ref, spin_ref, drift_ref, stiff_ref, ext_ref, out_ref, coef_ref, one, two, three):
    nazi, planes, rows, cells = ext_ref.shape
    own_rows = rows - 2 * OWN
    rad, azi = lax.axis_index("rad"), lax.axis_index("azi")
    lane = lax.broadcasted_iota(jnp.int32, (8, LANES), 1)
    wide = range(HALO, rows - HALO, 8)
    own = range(OWN, rows - OWN, 8)
    fill_coefficients(coef_ref, rad * own_rows - HALO, shift_ref, spin_ref, drift_ref, stiff_ref)

    def amounts(s):
        shift = coef_ref[11, s : s + 8, :].astype(jnp.int32)
        return shift // LANES, shift % LANES

    def rotate(here, behind, offsets):
        mixed = jnp.where(lane >= LANES - offsets, behind, here)
        return jnp.take_along_axis(mixed, lax.rem(lane - offsets + LANES, LANES), axis=1)

    stage(ext_ref, None, one, coef_ref, wide, 0.0, 1.0)
    stage(one, ext_ref, two, coef_ref, wide, 0.75, 0.25)
    stage(two, ext_ref, three, coef_ref, wide, 1.0 / 3.0, 2.0 / 3.0)
    for s in wide:
        hops, offsets = amounts(s)

        def shifted(p, carry):
            blocks = [three[b, p, s : s + 8, :] for b in range(nazi)]
            blocks = [rotate(blocks[b], blocks[b - 1], offsets) for b in range(nazi)]
            for bit in range(nazi.bit_length() - 1):
                taken = (hops // (1 << bit)) % 2 == 1
                blocks = [jnp.where(taken, blocks[b - (1 << bit)], blocks[b]) for b in range(nazi)]
            for b in range(nazi):
                one[b, p, s : s + 8, :] = blocks[b]
            return carry

        lax.fori_loop(0, planes, shifted, 0)

    stage(one, None, two, coef_ref, wide, 0.0, 1.0)
    stage(two, one, three, coef_ref, wide, 0.75, 0.25)
    stage(three, one, two, coef_ref, own, 1.0 / 3.0, 2.0 / 3.0)
    for s in own:
        hops, offsets = amounts(s)
        source = lax.rem(azi - hops + nazi, nazi)

        def final(p, carry):
            blocks = [two[b, p, s : s + 8, :] for b in range(nazi)]
            here, behind = blocks[0], blocks[-1]
            for b in range(1, nazi):
                here = jnp.where(source == b, blocks[b], here)
                behind = jnp.where(source == b, blocks[b - 1], behind)
            out_ref[p, s - OWN : s - OWN + 8, :] = rotate(here, behind, offsets)
            return carry

        lax.fori_loop(0, planes, final, 0)


def on_device(state, shifts, spin, drift, stiffness):
    fields, levels, rows, cells = state.shape
    planes = fields * levels
    nrad, nazi = lax.axis_size("rad"), lax.axis_size("azi")
    flat = state.reshape(planes, rows, cells)
    ext = gathered(flat, nrad, nazi)
    whole = pltpu.VMEM(ext.shape, jnp.float32)
    out = pl.pallas_call(
        compute_kernel,
        out_shape=jax.ShapeDtypeStruct(flat.shape, jnp.float32),
        in_specs=[pl.BlockSpec(memory_space=pltpu.VMEM)] * 5,
        out_specs=pl.BlockSpec(memory_space=pltpu.VMEM),
        scratch_shapes=[pltpu.VMEM((12, rows + 2 * OWN, LANES), jnp.float32), whole, whole, whole],
        compiler_params=pltpu.CompilerParams(vmem_limit_bytes=40 * 2**20),
    )(shifts[None], spin[None], drift[None], stiffness, ext)
    return out.reshape(state.shape)


def solution(mesh):
    in_specs = (P(None, None, "rad", "azi"), P(), P(), P(), P())
    out_specs = P(None, None, "rad", "azi")
    return jax.shard_map(
        on_device, mesh=mesh, in_specs=in_specs, out_specs=out_specs, check_vma=False
    )
```

time: 42.7 us -> 42.9 us (level)
  Pallas kernels: 38.8 us -> 41.1 us
  other arithmetic: 2.01 us -> 0 us
    pallas_call x1, Pallas kernels: 14 us -> 16.2 us  [on_device(): pl.pallas_call(compute_kernel, out_shape=jax.ShapeDtypeStruct(flat.shape,...]
    mul x1 -> x0, other arithmetic: 0.68 us -> none  [on_device(): half * stiffness]
    another operation x1 -> x0, other arithmetic: 0.67 us -> none  [on_device(): jnp.stack([(1.0 - 4.0 * c) * unit, c * unit, c - half * drift, c + half *...]
    broadcast_in_dim x1 -> x0, other arithmetic: 0.66 us -> none  [on_device(): shifts.astype(jnp.float32)[None]]
    unnamed x2 -> x10, local copies, waits for them, and re-layouts: 1.31 us -> 1.55 us
where the time goes in v2:
time: 42.9 us; the launch traced here: 42.7 us
  Pallas kernels  41.1 us (96%)
  local copies, waits for them, and re-layouts  1.55 us (4%)
    pallas_call x1, Pallas kernels, gathered(): pl.pallas_call(functools.partial(gather_kernel, nrad, nazi), out_shape=ja...  24.9 us
    pallas_call x1, Pallas kernels, on_device(): pl.pallas_call(compute_kernel, out_shape=jax.ShapeDtypeStruct(flat.shape,...  16.2 us
    unnamed x10, local copies, waits for them, and re-layouts  1.55 us

profile of v2, /device:TPU:1, one launch (start us, length us, event | category | flops | bytes accessed | tf_op | source)
XLA Modules:
  0.0 42.7 jit_solution(10188666152540192321)
XLA Ops:
  0.0 0.0 copy-start.1
  0.0 0.0 copy-start.4
  0.0 0.0 copy-start.3
  0.0 0.0 copy-start.2
  0.0 24.9 %shard_map.55.ext_ref = f32[4,20,48,128]{3,2,1,0:T(8,128)} custom-call(f32[20,16,128]{2,1,0:T(8,128)} %bitcast.8), custom_call_target="tpu_custom_call" | custom-call | tf_op jit(solution)/shard_map/pallas_call | solution.py:158
  24.9 0.0 copy-done.1
  24.9 0.0 copy-done.4
  24.9 0.0 copy-done.3
  24.9 0.0 copy-done.2
  24.9 0.0 copy-start
  25.0 1.5 %copy-done = f32[4,20,48,128]{3,2,1,0:T(8,128)S(1)} copy-done((f32[4,20,48,128]{3,2,1,0:T(8,128)S(1)}, f32[4,20,48,128]{3,2,1,0:T(8,128)}, u32[]{:S(2)}) %copy-start) | copy-done | bytes 1966104
  26.5 16.2 %shard_map.56 = f32[20,16,128]{2,1,0:T(8,128)} custom-call(s32[1,128]{1,0:T(1,128)S(1)} %bitcast.5, f32[1,128]{1,0:T(1,128)S(1)} %bitcast.6, f32[1,128]{1,0:T(1,128)S(1)} %bitcast.7, f32[4,128]{1,0:T(4,128)S(1)} %copy-done.1, f32[4,20,48,128]{3,2,1,0:T(8,128)S(1)} %copy-done), custom_call_target="tpu_custom_call" | custom-call | tf_op jit(solution)/shard_map/pallas_call | solution.py:320
Async XLA Ops:
  0.0 24.9 %copy-start.1 = (f32[4,128]{1,0:T(4,128)S(1)}, f32[4,128]{1,0:T(4,128)}, u32[]{:S(2)}) copy-start(f32[4,128]{1,0:T(4,128)} %stiff_ref.1) | copy-start | bytes 6148
  0.0 24.9 %copy-start.4 = (f32[128]{0:T(128)S(1)}, f32[128]{0:T(128)}, u32[]{:S(2)}) copy-start(f32[128]{0:T(128)} %param.8) | copy-start | bytes 1540
  0.0 24.9 %copy-start.3 = (f32[128]{0:T(128)S(1)}, f32[128]{0:T(128)}, u32[]{:S(2)}) copy-start(f32[128]{0:T(128)} %param.7) | copy-start | bytes 1540
  0.0 24.9 %copy-start.2 = (s32[128]{0:T(128)S(1)}, s32[128]{0:T(128)}, u32[]{:S(2)}) copy-start(s32[128]{0:T(128)} %param.6) | copy-start | bytes 1540
  24.9 1.5 %copy-start = (f32[4,20,48,128]{3,2,1,0:T(8,128)S(1)}, f32[4,20,48,128]{3,2,1,0:T(8,128)}, u32[]{:S(2)}) copy-start(f32[4,20,48,128]{3,2,1,0:T(8,128)} %shard_map.55.ext_ref) | copy-start | bytes 5898244

commit v3 on v2

--- a/solution.py
+++ b/solution.py
@@ -159,7 +159,7 @@
         functools.partial(gather_kernel, nrad, nazi),
         out_shape=jax.ShapeDtypeStruct((nazi, planes, rows + 2 * OWN, cells), jnp.float32),
         in_specs=[pl.BlockSpec(memory_space=pl.ANY)],
-        out_specs=pl.BlockSpec(memory_space=pl.ANY),
+        out_specs=pl.BlockSpec(memory_space=pltpu.VMEM),
         scratch_shapes=[
             pltpu.VMEM((planes, HALO, cells), jnp.float32),
             pltpu.SemaphoreType.DMA,
@@ -169,8 +169,17 @@
             pltpu.SemaphoreType.DMA((2, nazi)),
             pltpu.SemaphoreType.DMA((2, nazi)),
         ],
-        compiler_params=pltpu.CompilerParams(collective_id=0, has_side_effects=True),
+        compiler_params=pltpu.CompilerParams(
+            collective_id=0, has_side_effects=True, vmem_limit_bytes=20 * 2**20
+        ),
     )(x)
+
+
+def tiles_for(first, last):
+    starts = list(range(first, last - 6, 8))
+    if starts[-1] + 7 < last:
+        starts.append(last - 7)
+    return starts
 
 
 def stage(src, base, dst, coef, tiles, old, new):
@@ -207,6 +216,7 @@
                     return -cell(f, k - 1)
                 return cell(f, k + 1) - cell(f, k - 1)
 
+            done = {}
             for k in range(LEVELS):
                 rho, u, v, w, p = (around(f, k) for f in range(5))
                 div = (u[1] - u[2]) + (v[3] - v[4]) + vertical(3, k)
@@ -221,7 +231,9 @@
                     plane = f * LEVELS + k
                     if base is not None:
                         result = old * base[j, plane, s : s + 8, :] + new * result
-                    dst[j, plane, s : s + 8, :] = result
+                    done[plane] = result
+            for plane, result in done.items():
+                dst[j, plane, s : s + 8, :] = result
         return carry
 
     lax.fori_loop(0, nazi, body, 0)
@@ -261,8 +273,10 @@
     own_rows = rows - 2 * OWN
     rad, azi = lax.axis_index("rad"), lax.axis_index("azi")
     lane = lax.broadcasted_iota(jnp.int32, (8, LANES), 1)
-    wide = range(HALO, rows - HALO, 8)
-    own = range(OWN, rows - OWN, 8)
+
+    def rows_with(margin):
+        return tiles_for(OWN - margin, rows - OWN - 1 + margin)
+
     fill_coefficients(coef_ref, rad * own_rows - HALO, shift_ref, spin_ref, drift_ref, stiff_ref)
 
     def amounts(s):
@@ -273,10 +287,10 @@
         mixed = jnp.where(lane >= LANES - offsets, behind, here)
         return jnp.take_along_axis(mixed, lax.rem(lane - offsets + LANES, LANES), axis=1)
 
-    stage(ext_ref, None, one, coef_ref, wide, 0.0, 1.0)
-    stage(one, ext_ref, two, coef_ref, wide, 0.75, 0.25)
-    stage(two, ext_ref, three, coef_ref, wide, 1.0 / 3.0, 2.0 / 3.0)
-    for s in wide:
+    stage(ext_ref, None, one, coef_ref, rows_with(5), 0.0, 1.0)
+    stage(one, ext_ref, two, coef_ref, rows_with(4), 0.75, 0.25)
+    stage(two, ext_ref, three, coef_ref, rows_with(3), 1.0 / 3.0, 2.0 / 3.0)
+    for s in rows_with(3):
         hops, offsets = amounts(s)
 
         def shifted(p, carry):
@@ -291,10 +305,10 @@
 
         lax.fori_loop(0, planes, shifted, 0)
 
-    stage(one, None, two, coef_ref, wide, 0.0, 1.0)
-    stage(two, one, three, coef_ref, wide, 0.75, 0.25)
-    stage(three, one, two, coef_ref, own, 1.0 / 3.0, 2.0 / 3.0)
-    for s in own:
+    stage(one, None, two, coef_ref, rows_with(2), 0.0, 1.0)
+    stage(two, one, three, coef_ref, rows_with(1), 0.75, 0.25)
+    stage(three, one, two, coef_ref, rows_with(0), 1.0 / 3.0, 2.0 / 3.0)
+    for s in rows_with(0):
         hops, offsets = amounts(s)
         source = lax.rem(azi - hops + nazi, nazi)
 

time: 42.9 us -> 38.6 us (0.90)
  Pallas kernels: 41.1 us -> 37.4 us
  local copies, waits for them, and re-layouts: 1.55 us -> 0.97 us
    pallas_call x1, Pallas kernels: 16.2 us -> 13.9 us  [on_device(): pl.pallas_call(compute_kernel, out_shape=jax.ShapeDtypeStruct(flat.shape,...]
    pallas_call x1, Pallas kernels: 24.9 us -> 23.6 us  [gathered(): pl.pallas_call(functools.partial(gather_kernel, nrad, nazi), out_shape=ja...]
    unnamed x10, local copies, waits for them, and re-layouts: 1.55 us -> 0.97 us
where the time goes in v3:
time: 38.6 us; the launch traced here: 38.5 us
  Pallas kernels  37.4 us (97%)
  local copies, waits for them, and re-layouts  0.97 us (3%)
    pallas_call x1, Pallas kernels, gathered(): pl.pallas_call(functools.partial(gather_kernel, nrad, nazi), out_shape=ja...  23.6 us
    pallas_call x1, Pallas kernels, on_device(): pl.pallas_call(compute_kernel, out_shape=jax.ShapeDtypeStruct(flat.shape,...  13.9 us
    unnamed x10, local copies, waits for them, and re-layouts  0.97 us

profile of v3, /device:TPU:1, one launch (start us, length us, event | category | flops | bytes accessed | tf_op | source)
XLA Modules:
  0.0 38.5 jit_solution(9052942558849215815)
XLA Ops:
  0.0 0.0 copy-start.1
  0.0 0.0 copy-start.4
  0.0 0.0 copy-start.3
  0.0 0.0 copy-start.2
  0.0 0.0 copy-start
  0.0 0.9 %copy-done = f32[5,4,16,128]{3,2,1,0:T(8,128)S(1)} copy-done((f32[5,4,16,128]{3,2,1,0:T(8,128)S(1)}, f32[5,4,16,128]{3,2,1,0:T(8,128)}, u32[]{:S(2)}) %copy-start) | copy-done | bytes 163864
  1.0 23.6 %shard_map.55.ext_ref = f32[4,20,48,128]{3,2,1,0:T(8,128)S(1)} custom-call(f32[20,16,128]{2,1,0:T(8,128)S(1)} %bitcast.5), custom_call_target="tpu_custom_call" | custom-call | tf_op jit(solution)/shard_map/pallas_call | solution.py:158
  24.6 0.0 copy-done.1
  24.6 0.0 copy-done.4
  24.6 0.0 copy-done.3
  24.6 0.0 copy-done.2
  24.6 13.9 %shard_map.56 = f32[20,16,128]{2,1,0:T(8,128)} custom-call(s32[1,128]{1,0:T(1,128)S(1)} %bitcast.6, f32[1,128]{1,0:T(1,128)S(1)} %bitcast.7, f32[1,128]{1,0:T(1,128)S(1)} %bitcast.8, f32[4,128]{1,0:T(4,128)S(1)} %copy-done.1, f32[4,20,48,128]{3,2,1,0:T(8,128)S(1)} %shard_map.55.ext_ref), custom_call_target="tpu_custom_call" | custom-call | tf_op jit(solution)/shard_map/pallas_call | solution.py:334
Async XLA Ops:
  0.0 24.6 %copy-start.1 = (f32[4,128]{1,0:T(4,128)S(1)}, f32[4,128]{1,0:T(4,128)}, u32[]{:S(2)}) copy-start(f32[4,128]{1,0:T(4,128)} %stiff_ref.1) | copy-start | bytes 6148
  0.0 24.6 %copy-start.4 = (f32[128]{0:T(128)S(1)}, f32[128]{0:T(128)}, u32[]{:S(2)}) copy-start(f32[128]{0:T(128)} %param.8) | copy-start | bytes 1540
  0.0 24.6 %copy-start.3 = (f32[128]{0:T(128)S(1)}, f32[128]{0:T(128)}, u32[]{:S(2)}) copy-start(f32[128]{0:T(128)} %param.7) | copy-start | bytes 1540
  0.0 24.6 %copy-start.2 = (s32[128]{0:T(128)S(1)}, s32[128]{0:T(128)}, u32[]{:S(2)}) copy-start(s32[128]{0:T(128)} %param.6) | copy-start | bytes 1540
  0.0 1.0 %copy-start = (f32[5,4,16,128]{3,2,1,0:T(8,128)S(1)}, f32[5,4,16,128]{3,2,1,0:T(8,128)}, u32[]{:S(2)}) copy-start(f32[5,4,16,128]{3,2,1,0:T(8,128)} %param.5) | copy-start | bytes 491524

commit v4 on v3

--- a/solution.py
+++ b/solution.py
@@ -158,7 +158,7 @@
     return pl.pallas_call(
         functools.partial(gather_kernel, nrad, nazi),
         out_shape=jax.ShapeDtypeStruct((nazi, planes, rows + 2 * OWN, cells), jnp.float32),
-        in_specs=[pl.BlockSpec(memory_space=pl.ANY)],
+        in_specs=[pl.BlockSpec(memory_space=pltpu.HBM)],
         out_specs=pl.BlockSpec(memory_space=pltpu.VMEM),
         scratch_shapes=[
             pltpu.VMEM((planes, HALO, cells), jnp.float32),
@@ -277,6 +277,7 @@
     def rows_with(margin):
         return tiles_for(OWN - margin, rows - OWN - 1 + margin)
 
+    group = max(1, planes * 4 // max(nazi, 4))
     fill_coefficients(coef_ref, rad * own_rows - HALO, shift_ref, spin_ref, drift_ref, stiff_ref)
 
     def amounts(s):
@@ -303,7 +304,7 @@
                 one[b, p, s : s + 8, :] = blocks[b]
             return carry
 
-        lax.fori_loop(0, planes, shifted, 0)
+        lax.fori_loop(0, planes, shifted, 0, unroll=group)
 
     stage(one, None, two, coef_ref, rows_with(2), 0.0, 1.0)
     stage(two, one, three, coef_ref, rows_with(1), 0.75, 0.25)
@@ -321,7 +322,7 @@
             out_ref[p, s - OWN : s - OWN + 8, :] = rotate(here, behind, offsets)
             return carry
 
-        lax.fori_loop(0, planes, final, 0)
+        lax.fori_loop(0, planes, final, 0, unroll=group)
 
 
 def on_device(state, shifts, spin, drift, stiffness):

time: 38.6 us -> 30.9 us (0.80)
  Pallas kernels: 37.4 us -> 29.8 us
    pallas_call x1, Pallas kernels: 13.9 us -> 6.21 us  [on_device(): pl.pallas_call(compute_kernel, out_shape=jax.ShapeDtypeStruct(flat.shape,...]
where the time goes in v4:
time: 30.9 us; the launch traced here: 30.8 us
  Pallas kernels  29.8 us (96%)
  local copies, waits for them, and re-layouts  0.97 us (3%)
    pallas_call x1, Pallas kernels, gathered(): pl.pallas_call(functools.partial(gather_kernel, nrad, nazi), out_shape=ja...  23.6 us
    pallas_call x1, Pallas kernels, on_device(): pl.pallas_call(compute_kernel, out_shape=jax.ShapeDtypeStruct(flat.shape,...  6.21 us
    unnamed x10, local copies, waits for them, and re-layouts  0.97 us

profile of v4, /device:TPU:1, one launch (start us, length us, event | category | flops | bytes accessed | tf_op | source)
XLA Modules:
  0.0 30.8 jit_solution(1876208255174075002)
XLA Ops:
  0.0 0.0 copy-start.1
  0.0 0.0 copy-start.4
  0.0 0.0 copy-start.3
  0.0 0.0 copy-start.2
  0.0 0.0 copy-start
  0.0 0.9 %copy-done = f32[5,4,16,128]{3,2,1,0:T(8,128)S(1)} copy-done((f32[5,4,16,128]{3,2,1,0:T(8,128)S(1)}, f32[5,4,16,128]{3,2,1,0:T(8,128)}, u32[]{:S(2)}) %copy-start) | copy-done | bytes 163864
  1.0 23.6 %shard_map.55.ext_ref = f32[4,20,48,128]{3,2,1,0:T(8,128)S(1)} custom-call(f32[20,16,128]{2,1,0:T(8,128)S(1)} %bitcast.5), custom_call_target="tpu_custom_call" | custom-call | tf_op jit(solution)/shard_map/pallas_call | solution.py:158
  24.6 0.0 copy-done.1
  24.6 0.0 copy-done.4
  24.6 0.0 copy-done.3
  24.6 0.0 copy-done.2
  24.6 6.2 %shard_map.56 = f32[20,16,128]{2,1,0:T(8,128)} custom-call(s32[1,128]{1,0:T(1,128)S(1)} %bitcast.6, f32[1,128]{1,0:T(1,128)S(1)} %bitcast.7, f32[1,128]{1,0:T(1,128)S(1)} %bitcast.8, f32[4,128]{1,0:T(4,128)S(1)} %copy-done.1, f32[4,20,48,128]{3,2,1,0:T(8,128)S(1)} %shard_map.55.ext_ref), custom_call_target="tpu_custom_call" | custom-call | tf_op jit(solution)/shard_map/pallas_call | solution.py:335
Async XLA Ops:
  0.0 24.6 %copy-start.1 = (f32[4,128]{1,0:T(4,128)S(1)}, f32[4,128]{1,0:T(4,128)}, u32[]{:S(2)}) copy-start(f32[4,128]{1,0:T(4,128)} %stiff_ref.1) | copy-start | bytes 6148
  0.0 24.6 %copy-start.4 = (f32[128]{0:T(128)S(1)}, f32[128]{0:T(128)}, u32[]{:S(2)}) copy-start(f32[128]{0:T(128)} %param.8) | copy-start | bytes 1540
  0.0 24.6 %copy-start.3 = (f32[128]{0:T(128)S(1)}, f32[128]{0:T(128)}, u32[]{:S(2)}) copy-start(f32[128]{0:T(128)} %param.7) | copy-start | bytes 1540
  0.0 24.6 %copy-start.2 = (s32[128]{0:T(128)S(1)}, s32[128]{0:T(128)}, u32[]{:S(2)}) copy-start(s32[128]{0:T(128)} %param.6) | copy-start | bytes 1540
  0.0 1.0 %copy-start = (f32[5,4,16,128]{3,2,1,0:T(8,128)S(1)}, f32[5,4,16,128]{3,2,1,0:T(8,128)}, u32[]{:S(2)}) copy-start(f32[5,4,16,128]{3,2,1,0:T(8,128)} %param.5) | copy-start | bytes 491524

commit v5 on v4

v5 whole, which is shorter than its diff:
```python
import functools

import jax
import jax.numpy as jnp
from jax import lax
from jax.experimental import pallas as pl
from jax.experimental.pallas import tpu as pltpu
from jax.sharding import PartitionSpec as P

MESH = pl.DeviceIdType.MESH
STEPS = 2
HALO = 8
OWN = 16
LANES = 128
LEVELS = 4
time_step = 0.15
diffuse = 0.05


def tiles_for(first, last):
    starts = list(range(first, last - 6, 8))
    if starts[-1] + 7 < last:
        starts.append(last - 7)
    return starts


def stage(src, base, dst, coef, tiles, old, new):
    nazi = src.shape[0]
    lane = lax.broadcasted_iota(jnp.int32, (LEVELS, 8, LANES), 2)
    at_end, at_start = lane == LANES - 1, lane == 0

    def body(j, carry):
        before = lax.rem(j + nazi - 1, nazi)
        after = lax.rem(j + 1, nazi)
        for s in tiles:
            c0, d, ga, gb, h, s2, s5 = (coef[i, s : s + 8, :] for i in range(7))
            stiff = coef[7 : 7 + LEVELS, s : s + 8, :]

            def around(f):
                p = slice(f * LEVELS, (f + 1) * LEVELS)
                c = src[j, p, s : s + 8, :]
                up, lo = src[j, p, s + 1 : s + 9, :], src[j, p, s - 1 : s + 7, :]
                be = pltpu.roll(jnp.where(at_end, src[before, p, s : s + 8, :], c), 1, 2)
                ah = pltpu.roll(jnp.where(at_start, src[after, p, s : s + 8, :], c), LANES - 1, 2)
                return c, up, lo, ah, be

            def rest(parts):
                c, up, lo, ah, be = parts
                return c0 * c + d * (up + lo) + (ga * ah + gb * be)

            def vertical(c):
                middle = c[2:] - c[:-2]
                return jnp.concatenate([c[1:2], middle, -c[LEVELS - 2 : LEVELS - 1]], axis=0)

            rho, u, v, w, p = (around(f) for f in range(5))
            div = (u[1] - u[2]) + (v[3] - v[4]) + vertical(w[0])
            results = (
                rest(rho) - h * div,
                rest(u) + s2 * v[0] - h * (p[1] - p[2]),
                rest(v) - s5 * u[0] - h * (p[3] - p[4]),
                rest(w) - h * vertical(p[0]),
                rest(p) - stiff * div,
            )
            for f, result in enumerate(results):
                planes = slice(f * LEVELS, (f + 1) * LEVELS)
                if base is not None:
                    result = old * base[j, planes, s : s + 8, :] + new * result
                dst[j, planes, s : s + 8, :] = result
        return carry

    lax.fori_loop(0, nazi, body, 0)


def fill_coefficients(coef, first, shift_ref, spin_ref, drift_ref, stiff_ref):
    count = coef.shape[1] - 2 * HALO
    shape = (count, spin_ref.shape[1])
    radius = lax.broadcasted_iota(jnp.int32, shape, 0) + first
    match = radius == lax.broadcasted_iota(jnp.int32, shape, 1)

    def column(values):
        picked = jnp.sum(jnp.where(match, values, 0.0), axis=1, keepdims=True)
        return jnp.broadcast_to(picked, (count, LANES))

    c = time_step * diffuse
    half = 0.5 * time_step
    inside = column(jnp.ones((1, shape[1]), jnp.float32))
    spin, drift = column(spin_ref[...]), column(drift_ref[...])
    values = [
        (1.0 - 4.0 * c) * inside,
        c * inside,
        c * inside - half * drift,
        c * inside + half * drift,
        half * inside,
        2.0 * time_step * spin,
        half * spin,
    ]
    values += [half * column(stiff_ref[k : k + 1, :]) for k in range(LEVELS)]
    values.append(column(shift_ref[...].astype(jnp.float32)))
    for i, value in enumerate(values):
        coef[i, HALO : HALO + count, :] = value


def first_kernel(
    nrad, nazi, shift_ref, spin_ref, drift_ref, stiff_ref, x_ref, sect_ref, coef_ref,
    ext_ref, one, two, own_sem, z_send, z_recv, h_send, h_recv,
):
    rad, azi = lax.axis_index("rad"), lax.axis_index("azi")
    rows = x_ref.shape[1]
    odd = lax.rem(rad, 2)
    has_left, has_right = azi > 0, azi < nazi - 1

    def upper(c):
        return 1 - lax.rem(odd + c, 2)

    def peer(c):
        return rad + (1 - 2 * odd) * (1 - 2 * c)

    has_other = jnp.logical_and(peer(1) >= 0, peer(1) < nrad)

    def half_at(c, offset):
        return pl.ds(pl.multiple_of(HALO * upper(c) + offset, HALO), HALO)

    barrier = pltpu.get_barrier_semaphore()
    expected = 1
    pl.semaphore_signal(barrier, inc=1, device_id=(peer(0), azi), device_id_type=MESH)
    for present, to_rad, to_azi in ((has_left, rad, azi - 1), (has_right, rad, azi + 1), (has_other, peer(1), azi)):
        expected = expected + present.astype(jnp.int32)

        @pl.when(present)
        def _():
            pl.semaphore_signal(barrier, inc=1, device_id=(to_rad, to_azi), device_id_type=MESH)

    own = pltpu.make_async_copy(x_ref, ext_ref.at[azi, :, pl.ds(OWN, rows)], own_sem)
    own.start()
    fill_coefficients(coef_ref, rad * rows - HALO, shift_ref, spin_ref, drift_ref, stiff_ref)

    @pl.when(jnp.logical_not(has_other))
    def _():
        start = pl.multiple_of(OWN - HALO + (HALO + rows) * upper(1), HALO)
        for b in range(nazi):
            ext_ref[b, :, pl.ds(start, HALO), :] = jnp.zeros((x_ref.shape[0], HALO, LANES), jnp.float32)

    pl.semaphore_wait(barrier, expected)

    def z_copy(side, t, c, block, src):
        return pltpu.make_async_remote_copy(
            src_ref=src,
            dst_ref=ext_ref.at[block, :, half_at(c, OWN)],
            send_sem=z_send.at[side, t, c],
            recv_sem=z_recv.at[side, t, c],
            device_id=(rad, azi + 1 if side == 0 else azi - 1),
            device_id_type=MESH,
        )

    def along(side, t, c):
        block = azi - t if side == 0 else azi + t
        src = x_ref.at[:, half_at(c, 0)] if t == 0 else ext_ref.at[block, :, half_at(c, OWN)]
        return z_copy(side, t, c, block, src)

    def came(side, t):
        return azi - 1 - t if side == 0 else azi + 1 + t

    def arrived(side, t, c):
        return z_copy(side, t, c, came(side, t), x_ref.at[:, half_at(c, 0)])

    def last(side):
        return azi if side == 0 else nazi - 1 - azi

    def sends(side, t):
        return jnp.logical_and(t <= last(side), has_right if side == 0 else has_left)

    def arrives(side, t):
        return came(side, t) >= 0 if side == 0 else came(side, t) < nazi

    def radial(c, block, src):
        there = pl.multiple_of(OWN + rows - (HALO + rows) * upper(c), HALO)
        return pltpu.make_async_remote_copy(
            src_ref=src,
            dst_ref=ext_ref.at[block, :, pl.ds(there, HALO)],
            send_sem=h_send.at[c, block],
            recv_sem=h_recv.at[c, block],
            device_id=(peer(c), azi),
            device_id_type=MESH,
        )

    def radial_in(c, block):
        here = pl.multiple_of(OWN - HALO + (HALO + rows) * upper(c), HALO)
        return pltpu.make_async_remote_copy(
            src_ref=x_ref.at[:, half_at(c, 0)],
            dst_ref=ext_ref.at[block, :, pl.ds(here, HALO)],
            send_sem=h_send.at[c, block],
            recv_sem=h_recv.at[c, block],
            device_id=(peer(c), azi),
            device_id_type=MESH,
        )

    def pass_on(c, block, own_block=False):
        src = x_ref.at[:, half_at(c, 0)] if own_block else ext_ref.at[block, :, half_at(c, OWN)]
        if c == 0:
            radial(c, block, src).start()
        else:

            @pl.when(has_other)
            def _():
                radial(c, block, src).start()

    def send(side, t):
        @pl.when(sends(side, t))
        def _():
            along(side, t, 0).start()

            @pl.when(last(side) == t)
            def _():
                along(side, 0, 1).start()

    def step(t, c):
        for side in range(2):

            @pl.when(arrives(side, t))
            def _():
                arrived(side, t, c).wait_recv()
                if c == 0:
                    send(side, t + 1)
                else:

                    @pl.when(sends(side, t + 1))
                    def _():
                        along(side, t + 1, c).start()

                pass_on(c, came(side, t))

    def both(even_rows, odd_rows, src, base, dst, old, new):
        for parity, (start, end) in enumerate((even_rows, odd_rows)):

            @pl.when(odd == parity)
            def _():
                stage(src, base, dst, coef_ref, tiles_for(start, end), old, new)

    low, high, middle = OWN, OWN + rows - 1, OWN + HALO
    third = (1.0 / 3.0, 2.0 / 3.0)

    for side in range(2):
        send(side, 0)
    pass_on(0, azi, True)
    pass_on(1, azi, True)
    for t in range(nazi - 1):
        step(t, 0)
    own.wait()
    for b in range(nazi):
        radial_in(0, b).wait_recv()
    for t in range(max(3, nazi - 1)):
        if t == 0:
            both((middle + 1, high + 5), (low - 5, middle - 2), ext_ref, None, one, 0.0, 1.0)
        if t == 1:
            both((middle + 2, high + 4), (low - 4, middle - 3), one, ext_ref, two, 0.75, 0.25)
        if t == 2:
            both((middle + 3, high + 3), (low - 3, middle - 4), two, ext_ref, sect_ref, *third)
        if t < nazi - 1:
            step(t, 1)

    @pl.when(has_other)
    def _():
        for b in range(nazi):
            radial_in(1, b).wait_recv()

    both((low - 5, middle), (middle - 1, high + 5), ext_ref, None, one, 0.0, 1.0)
    both((low - 4, middle + 1), (middle - 2, high + 4), one, ext_ref, two, 0.75, 0.25)
    both((low - 3, middle + 2), (middle - 3, high + 3), two, ext_ref, sect_ref, *third)

    for c in range(2):
        for t in range(nazi - 1):
            for side in range(2):

                @pl.when(sends(side, t))
                def _():
                    along(side, t, c).wait_send()

    for b in range(nazi):
        radial_in(0, b).wait_send()

    @pl.when(has_other)
    def _():
        for b in range(nazi):
            radial_in(1, b).wait_send()


def second_kernel(sect_ref, coef_ref, out_ref, one, two, three):
    nazi, planes, rows, cells = sect_ref.shape
    azi = lax.axis_index("azi")
    lane = lax.broadcasted_iota(jnp.int32, (8, LANES), 1)

    def rows_with(margin):
        return tiles_for(OWN - margin, rows - OWN - 1 + margin)

    group = max(1, planes * 4 // max(nazi, 4))

    def amounts(s):
        shift = coef_ref[11, s : s + 8, :].astype(jnp.int32)
        return shift // LANES, shift % LANES

    def rotate(here, behind, offsets):
        mixed = jnp.where(lane >= LANES - offsets, behind, here)
        return jnp.take_along_axis(mixed, lax.rem(lane - offsets + LANES, LANES), axis=1)

    for s in rows_with(3):
        hops, offsets = amounts(s)

        def shifted(p, carry):
            blocks = [sect_ref[b, p, s : s + 8, :] for b in range(nazi)]
            blocks = [rotate(blocks[b], blocks[b - 1], offsets) for b in range(nazi)]
            for bit in range(nazi.bit_length() - 1):
                taken = (hops // (1 << bit)) % 2 == 1
                blocks = [jnp.where(taken, blocks[b - (1 << bit)], blocks[b]) for b in range(nazi)]
            for b in range(nazi):
                one[b, p, s : s + 8, :] = blocks[b]
            return carry

        lax.fori_loop(0, planes, shifted, 0, unroll=group)

    stage(one, None, two, coef_ref, rows_with(2), 0.0, 1.0)
    stage(two, one, three, coef_ref, rows_with(1), 0.75, 0.25)
    stage(three, one, two, coef_ref, rows_with(0), 1.0 / 3.0, 2.0 / 3.0)
    for s in rows_with(0):
        hops, offsets = amounts(s)
        source = lax.rem(azi - hops + nazi, nazi)

        def final(p, carry):
            blocks = [two[b, p, s : s + 8, :] for b in range(nazi)]
            here, behind = blocks[0], blocks[-1]
            for b in range(1, nazi):
                here = jnp.where(source == b, blocks[b], here)
                behind = jnp.where(source == b, blocks[b - 1], behind)
            out_ref[p, s - OWN : s - OWN + 8, :] = rotate(here, behind, offsets)
            return carry

        lax.fori_loop(0, planes, final, 0, unroll=group)


def on_device(state, shifts, spin, drift, stiffness):
    fields, levels, rows, cells = state.shape
    planes = fields * levels
    nrad, nazi = lax.axis_size("rad"), lax.axis_size("azi")
    flat = state.reshape(planes, rows, cells)
    whole_shape = (nazi, planes, rows + 2 * OWN, cells)
    coef_shape = (12, rows + 2 * OWN, cells)
    whole = pltpu.VMEM(whole_shape, jnp.float32)
    vmem = pl.BlockSpec(memory_space=pltpu.VMEM)
    dma = pltpu.SemaphoreType.DMA
    sect, coef = pl.pallas_call(
        functools.partial(first_kernel, nrad, nazi),
        out_shape=(
            jax.ShapeDtypeStruct(whole_shape, jnp.float32),
            jax.ShapeDtypeStruct(coef_shape, jnp.float32),
        ),
        in_specs=[vmem] * 4 + [pl.BlockSpec(memory_space=pl.ANY)],
        out_specs=(vmem, vmem),
        scratch_shapes=[
            whole,
            whole,
            whole,
            dma,
            dma((2, nazi, 2)),
            dma((2, nazi, 2)),
            dma((2, nazi)),
            dma((2, nazi)),
        ],
        compiler_params=pltpu.CompilerParams(
            collective_id=0, has_side_effects=True, vmem_limit_bytes=40 * 2**20
        ),
    )(shifts[None], spin[None], drift[None], stiffness, flat)
    out = pl.pallas_call(
        second_kernel,
        out_shape=jax.ShapeDtypeStruct(flat.shape, jnp.float32),
        in_specs=[vmem, vmem],
        out_specs=vmem,
        scratch_shapes=[whole, whole, whole],
        compiler_params=pltpu.CompilerParams(vmem_limit_bytes=40 * 2**20),
    )(sect, coef)
    return out.reshape(state.shape)


def solution(mesh):
    in_specs = (P(None, None, "rad", "azi"), P(), P(), P(), P())
    out_specs = P(None, None, "rad", "azi")
    return jax.shard_map(
        on_device, mesh=mesh, in_specs=in_specs, out_specs=out_specs, check_vma=False
    )
```

time: 30.9 us -> 34.3 us (1.11)
  local copies, waits for them, and re-layouts: 0.97 us -> 3.56 us
  Pallas kernels: 29.8 us -> 30.6 us
    unnamed x10, local copies, waits for them, and re-layouts: 0.97 us -> 3.56 us
    pallas_call x2, Pallas kernels: 29.8 us -> 30.6 us  [the longest x1 27.2 us: on_device(): pl.pallas_call(functools.partial(first_kernel, nrad, nazi), out_shape=(ja...]
where the time goes in v5:
time: 34.3 us; the launch traced here: 34.2 us
  Pallas kernels  30.6 us (89%)
  local copies, waits for them, and re-layouts  3.56 us (10%)
    pallas_call x1, Pallas kernels, on_device(): pl.pallas_call(functools.partial(first_kernel, nrad, nazi), out_shape=(ja...  27.2 us
    unnamed x10, local copies, waits for them, and re-layouts  3.56 us
    pallas_call x1, Pallas kernels, on_device(): pl.pallas_call(second_kernel, out_shape=jax.ShapeDtypeStruct(flat.shape,...  3.42 us

profile of v5, /device:TPU:1, one launch (start us, length us, event | category | flops | bytes accessed | tf_op | source)
XLA Modules:
  0.0 34.2 jit_solution(5062084659021677126)
XLA Ops:
  0.0 0.0 copy-start
  0.0 0.9 %copy-done = f32[5,4,16,128]{3,2,1,0:T(8,128)S(1)} copy-done((f32[5,4,16,128]{3,2,1,0:T(8,128)S(1)}, f32[5,4,16,128]{3,2,1,0:T(8,128)}, u32[]{:S(2)}) %copy-start) | copy-done | bytes 163864
  0.9 0.0 copy-start.1
  0.9 0.7 %copy-done.1 = f32[4,128]{1,0:T(4,128)S(1)} copy-done((f32[4,128]{1,0:T(4,128)S(1)}, f32[4,128]{1,0:T(4,128)}, u32[]{:S(2)}) %copy-start.1) | copy-done | bytes 2072
  1.6 0.0 copy-start.2
  1.6 0.7 %copy-done.2 = s32[128]{0:T(128)S(1)} copy-done((s32[128]{0:T(128)S(1)}, s32[128]{0:T(128)}, u32[]{:S(2)}) %copy-start.2) | copy-done | bytes 536
  2.3 0.0 copy-start.3
  2.3 0.7 %copy-done.3 = f32[128]{0:T(128)S(1)} copy-done((f32[128]{0:T(128)S(1)}, f32[128]{0:T(128)}, u32[]{:S(2)}) %copy-start.3) | copy-done | bytes 536
  2.9 0.0 copy-start.4
  2.9 0.7 %copy-done.4 = f32[128]{0:T(128)S(1)} copy-done((f32[128]{0:T(128)S(1)}, f32[128]{0:T(128)}, u32[]{:S(2)}) %copy-start.4) | copy-done | bytes 536
  3.6 27.2 %shard_map.55 = (f32[4,20,48,128]{3,2,1,0:T(8,128)S(1)}, f32[12,48,128]{2,1,0:T(8,128)S(1)}) custom-call(s32[1,128]{1,0:T(1,128)S(1)} %bitcast.6, f32[1,128]{1,0:T(1,128)S(1)} %bitcast.7, f32[1,128]{1,0:T(1,128)S(1)} %bitcast.8, f32[4,128]{1,0:T(4,128)S(1)} %copy-done.1, f32[20,16,128]{2,1,0:T(8,128)S(1)} %bitcast.5), custom_call_target="tpu_custom_call" | custom-call | tf_op jit(solution)/shard_map/pallas_call | solution.py:349
  30.7 3.4 %shard_map.56 = f32[20,16,128]{2,1,0:T(8,128)} custom-call(f32[4,20,48,128]{3,2,1,0:T(8,128)S(1)} %get-tuple-element.7.sect_ref, f32[12,48,128]{2,1,0:T(8,128)S(1)} %get-tuple-element.8.coef_ref), custom_call_target="tpu_custom_call" | custom-call | tf_op jit(solution)/shard_map/pallas_call | solution.py:371
Async XLA Ops:
  0.0 0.9 %copy-start = (f32[5,4,16,128]{3,2,1,0:T(8,128)S(1)}, f32[5,4,16,128]{3,2,1,0:T(8,128)}, u32[]{:S(2)}) copy-start(f32[5,4,16,128]{3,2,1,0:T(8,128)} %param.5) | copy-start | bytes 491524
  0.9 0.7 %copy-start.1 = (f32[4,128]{1,0:T(4,128)S(1)}, f32[4,128]{1,0:T(4,128)}, u32[]{:S(2)}) copy-start(f32[4,128]{1,0:T(4,128)} %stiff_ref.1) | copy-start | bytes 6148
  1.6 0.7 %copy-start.2 = (s32[128]{0:T(128)S(1)}, s32[128]{0:T(128)}, u32[]{:S(2)}) copy-start(s32[128]{0:T(128)} %param.6) | copy-start | bytes 1540
  2.3 0.7 %copy-start.3 = (f32[128]{0:T(128)S(1)}, f32[128]{0:T(128)}, u32[]{:S(2)}) copy-start(f32[128]{0:T(128)} %param.7) | copy-start | bytes 1540
  2.9 0.7 %copy-start.4 = (f32[128]{0:T(128)S(1)}, f32[128]{0:T(128)}, u32[]{:S(2)}) copy-start(f32[128]{0:T(128)} %param.8) | copy-start | bytes 1540

commit v6 on v4

--- a/solution.py
+++ b/solution.py
@@ -172,7 +172,7 @@
         compiler_params=pltpu.CompilerParams(
             collective_id=0, has_side_effects=True, vmem_limit_bytes=20 * 2**20
         ),
-    )(x)
+    )(pltpu.with_memory_space_constraint(x, pltpu.HBM))
 
 
 def tiles_for(first, last):
@@ -236,7 +236,7 @@
                 dst[j, plane, s : s + 8, :] = result
         return carry
 
-    lax.fori_loop(0, nazi, body, 0)
+    lax.fori_loop(0, nazi, body, 0, unroll=2)
 
 
 def fill_coefficients(coef, first, shift_ref, spin_ref, drift_ref, stiff_ref):

time: 30.9 us -> 29.6 us (0.958)
  local copies, waits for them, and re-layouts: 0.97 us -> 0.02 us
  Pallas kernels: 29.8 us -> 29.4 us
    unnamed x10 -> x8, local copies, waits for them, and re-layouts: 0.97 us -> 0.02 us
    pallas_call x1, Pallas kernels: 6.21 us -> 5.56 us  [on_device(): pl.pallas_call(compute_kernel, out_shape=jax.ShapeDtypeStruct(flat.shape,...]
where the time goes in v6:
time: 29.6 us; the launch traced here: 29.4 us
  Pallas kernels  29.4 us (99%)
    pallas_call x1, Pallas kernels, gathered(): pl.pallas_call(functools.partial(gather_kernel, nrad, nazi), out_shape=ja...  23.8 us
    pallas_call x1, Pallas kernels, on_device(): pl.pallas_call(compute_kernel, out_shape=jax.ShapeDtypeStruct(flat.shape,...  5.56 us

profile of v6, /device:TPU:1, one launch (start us, length us, event | category | flops | bytes accessed | tf_op | source)
XLA Modules:
  0.0 29.4 jit_solution(12019897095022947766)
XLA Ops:
  0.0 0.0 copy-start
  0.0 0.0 copy-start.3
  0.0 0.0 copy-start.2
  0.0 0.0 copy-start.1
  0.0 23.8 %shard_map.55.ext_ref = f32[4,20,48,128]{3,2,1,0:T(8,128)S(1)} custom-call(f32[20,16,128]{2,1,0:T(8,128)} %bitcast.8), custom_call_target="tpu_custom_call" | custom-call | tf_op jit(solution)/shard_map/pallas_call | solution.py:158
  23.9 0.0 copy-done
  23.9 0.0 copy-done.3
  23.9 0.0 copy-done.2
  23.9 0.0 copy-done.1
  23.9 5.6 %shard_map.56 = f32[20,16,128]{2,1,0:T(8,128)} custom-call(s32[1,128]{1,0:T(1,128)S(1)} %bitcast.5, f32[1,128]{1,0:T(1,128)S(1)} %bitcast.6, f32[1,128]{1,0:T(1,128)S(1)} %bitcast.7, f32[4,128]{1,0:T(4,128)S(1)} %copy-done, f32[4,20,48,128]{3,2,1,0:T(8,128)S(1)} %shard_map.55.ext_ref), custom_call_target="tpu_custom_call" | custom-call | tf_op jit(solution)/shard_map/pallas_call | solution.py:335
Async XLA Ops:
  0.0 23.9 %copy-start = (f32[4,128]{1,0:T(4,128)S(1)}, f32[4,128]{1,0:T(4,128)}, u32[]{:S(2)}) copy-start(f32[4,128]{1,0:T(4,128)} %stiff_ref.1) | copy-start | bytes 6148
  0.0 23.9 %copy-start.3 = (f32[128]{0:T(128)S(1)}, f32[128]{0:T(128)}, u32[]{:S(2)}) copy-start(f32[128]{0:T(128)} %param.8) | copy-start | bytes 1540
  0.0 23.9 %copy-start.2 = (f32[128]{0:T(128)S(1)}, f32[128]{0:T(128)}, u32[]{:S(2)}) copy-start(f32[128]{0:T(128)} %param.7) | copy-start | bytes 1540
  0.0 23.9 %copy-start.1 = (s32[128]{0:T(128)S(1)}, s32[128]{0:T(128)}, u32[]{:S(2)}) copy-start(s32[128]{0:T(128)} %param.6) | copy-start | bytes 1540

commit v7 on v6

--- a/solution.py
+++ b/solution.py
@@ -17,18 +17,23 @@
 diffuse = 0.05
 
 
-def gather_kernel(nrad, nazi, x_ref, ext_ref, zeros, own_sem, z_send, z_recv, h_send, h_recv, edge_sem):
+def gather_kernel(nrad, nazi, x_ref, ext_ref, zeros, own_sem, z_send, z_recv, h_send, h_recv, edge_sem, ready):
     rad, azi = lax.axis_index("rad"), lax.axis_index("azi")
     rows = x_ref.shape[1]
     has_low, has_high = rad > 0, rad < nrad - 1
 
     has_left, has_right = azi > 0, azi < nazi - 1
-    neighbours = ((has_left, rad, azi - 1), (has_right, rad, azi + 1), (has_low, rad - 1, azi), (has_high, rad + 1, azi))
+    half = x_ref.shape[0] // 2
+    everywhere = ((has_left, rad, azi - 1), (has_right, rad, azi + 1), (has_low, rad - 1, azi), (has_high, rad + 1, azi))
 
     barrier = pltpu.get_barrier_semaphore()
     expected = 0
-    for present, to_rad, to_azi in neighbours:
-        expected = expected + present.astype(jnp.int32)
+    for i, (present, to_rad, to_azi) in enumerate(everywhere):
+        if i == 0:
+            expected = expected + present.astype(jnp.int32)
+            continue
+        if i > 1:
+            expected = expected + present.astype(jnp.int32)
 
         @pl.when(present)
         def _():
@@ -39,72 +44,87 @@
     zeros[...] = jnp.zeros_like(zeros)
     pl.semaphore_wait(barrier, expected)
 
-    def along(side, t):
-        block = azi - t if side == 0 else azi + t
-        src = x_ref if t == 0 else ext_ref.at[block, :, pl.ds(OWN, rows)]
+    @pl.when(has_left)
+    def _():
+        pl.semaphore_signal(ready, inc=1, device_id=(rad, azi - 1), device_id_type=MESH)
+
+    def planes(c):
+        return pl.ds(c * half, half)
+
+    def z_copy(side, t, c, block, src):
         return pltpu.make_async_remote_copy(
             src_ref=src,
-            dst_ref=ext_ref.at[block, :, pl.ds(OWN, rows)],
-            send_sem=z_send.at[side, t],
-            recv_sem=z_recv.at[side, t],
+            dst_ref=ext_ref.at[block, planes(c), pl.ds(OWN, rows)],
+            send_sem=z_send.at[side, t, c],
+            recv_sem=z_recv.at[side, t, c],
             device_id=(rad, azi + 1 if side == 0 else azi - 1),
             device_id_type=MESH,
         )
+
+    def along(side, t, c):
+        block = azi - t if side == 0 else azi + t
+        src = x_ref.at[planes(c)] if t == 0 else ext_ref.at[block, planes(c), pl.ds(OWN, rows)]
+        return z_copy(side, t, c, block, src)
 
     def sends(side, t):
         if side == 0:
             return jnp.logical_and(azi - t >= 0, has_right)
         return jnp.logical_and(azi + t < nazi, has_left)
 
+    def came(side, t):
+        return azi - 1 - t if side == 0 else azi + 1 + t
+
     def arrives(side, t):
-        return azi - 1 - t >= 0 if side == 0 else azi + 1 + t < nazi
-
-    def arrived(side, t):
-        block = azi - 1 - t if side == 0 else azi + 1 + t
-        return pltpu.make_async_remote_copy(
-            src_ref=x_ref,
-            dst_ref=ext_ref.at[block, :, pl.ds(OWN, rows)],
-            send_sem=z_send.at[side, t],
-            recv_sem=z_recv.at[side, t],
-            device_id=(rad, azi + 1 if side == 0 else azi - 1),
-            device_id_type=MESH,
-        )
-
-    def radial(to, block, own_block):
+        return came(side, t) >= 0 if side == 0 else came(side, t) < nazi
+
+    def arrived(side, t, c):
+        return z_copy(side, t, c, came(side, t), x_ref.at[planes(c)])
+
+    def radial(to, block, c, own_block):
         if to == 0:
             start, there = 0, OWN + rows
         else:
             start, there = rows - HALO, OWN - HALO
-        src = x_ref.at[:, pl.ds(start, HALO)] if own_block else ext_ref.at[block, :, pl.ds(OWN + start, HALO)]
+        if own_block:
+            src = x_ref.at[planes(c), pl.ds(start, HALO)]
+        else:
+            src = ext_ref.at[block, planes(c), pl.ds(OWN + start, HALO)]
         return pltpu.make_async_remote_copy(
             src_ref=src,
-            dst_ref=ext_ref.at[block, :, pl.ds(there, HALO)],
-            send_sem=h_send.at[to, block],
-            recv_sem=h_recv.at[to, block],
+            dst_ref=ext_ref.at[block, planes(c), pl.ds(there, HALO)],
+            send_sem=h_send.at[to, block, c],
+            recv_sem=h_recv.at[to, block, c],
             device_id=(rad - 1 if to == 0 else rad + 1, azi),
             device_id_type=MESH,
         )
 
-    def pass_on(block, own_block=False):
+    def pass_on(block, c, own_block=False):
         @pl.when(has_low)
         def _():
-            radial(0, block, own_block).start()
+            radial(0, block, c, own_block).start()
 
         @pl.when(has_high)
         def _():
-            radial(1, block, own_block).start()
+            radial(1, block, c, own_block).start()
 
     def edge(b, side):
         start = OWN - HALO if side == 0 else OWN + rows
         return pltpu.make_async_copy(zeros, ext_ref.at[b, :, pl.ds(start, HALO)], edge_sem.at[side, b])
 
-    for side in range(2):
-
-        @pl.when(sends(side, 0))
-        def _():
-            along(side, 0).start()
-
-    pass_on(azi, True)
+    @pl.when(has_left)
+    def _():
+        for c in range(2):
+            along(1, 0, c).start()
+
+    for c in range(2):
+        pass_on(azi, c, True)
+
+    @pl.when(has_right)
+    def _():
+        pl.semaphore_wait(ready, 1)
+        for c in range(2):
+            along(0, 0, c).start()
+
     for side, missing in enumerate((has_low, has_high)):
 
         @pl.when(jnp.logical_not(missing))
@@ -113,17 +133,17 @@
                 edge(b, side).start()
 
     for t in range(nazi - 1):
-        for side in range(2):
+        for c, side in ((0, 0), (0, 1), (1, 0), (1, 1)):
 
             @pl.when(arrives(side, t))
             def _():
-                arrived(side, t).wait_recv()
+                arrived(side, t, c).wait_recv()
 
                 @pl.when(sends(side, t + 1))
                 def _():
-                    along(side, t + 1).start()
-
-                pass_on(azi - 1 - t if side == 0 else azi + 1 + t)
+                    along(side, t + 1, c).start()
+
+                pass_on(came(side, t), c)
 
     for side, missing in enumerate((has_low, has_high)):
 
@@ -138,19 +158,22 @@
 
             @pl.when(sends(side, t))
             def _():
-                along(side, t).wait_send()
+                for c in range(2):
+                    along(side, t, c).wait_send()
 
     @pl.when(has_low)
     def _():
         for b in range(nazi):
-            radial(0, b, False).wait_send()
-            radial(1, b, False).wait_recv()
+            for c in range(2):
+                radial(0, b, c, False).wait_send()
+                radial(1, b, c, False).wait_recv()
 
     @pl.when(has_high)
     def _():
         for b in range(nazi):
-            radial(1, b, False).wait_send()
-            radial(0, b, False).wait_recv()
+            for c in range(2):
+                radial(1, b, c, False).wait_send()
+                radial(0, b, c, False).wait_recv()
 
 
 def gathered(x, nrad, nazi):
@@ -163,11 +186,12 @@
         scratch_shapes=[
             pltpu.VMEM((planes, HALO, cells), jnp.float32),
             pltpu.SemaphoreType.DMA,
+            pltpu.SemaphoreType.DMA((2, nazi, 2)),
+            pltpu.SemaphoreType.DMA((2, nazi, 2)),
+            pltpu.SemaphoreType.DMA((2, nazi, 2)),
+            pltpu.SemaphoreType.DMA((2, nazi, 2)),
             pltpu.SemaphoreType.DMA((2, nazi)),
-            pltpu.SemaphoreType.DMA((2, nazi)),
-            pltpu.SemaphoreType.DMA((2, nazi)),
-            pltpu.SemaphoreType.DMA((2, nazi)),
-            pltpu.SemaphoreType.DMA((2, nazi)),
+            pltpu.SemaphoreType.REGULAR,
         ],
         compiler_params=pltpu.CompilerParams(
             collective_id=0, has_side_effects=True, vmem_limit_bytes=20 * 2**20
@@ -236,7 +260,7 @@
                 dst[j, plane, s : s + 8, :] = result
         return carry
 
-    lax.fori_loop(0, nazi, body, 0, unroll=2)
+    lax.fori_loop(0, nazi, body, 0, unroll=4)
 
 
 def fill_coefficients(coef, first, shift_ref, spin_ref, drift_ref, stiff_ref):

time: 29.6 us -> 27 us (0.912)
  Pallas kernels: 29.4 us -> 26.8 us
    pallas_call x1, Pallas kernels: 23.8 us -> 21.4 us  [gathered(): pl.pallas_call(functools.partial(gather_kernel, nrad, nazi), out_shape=ja...]
where the time goes in v7:
time: 27 us; the launch traced here: 26.9 us
  Pallas kernels  26.8 us (99%)
    pallas_call x1, Pallas kernels, gathered(): pl.pallas_call(functools.partial(gather_kernel, nrad, nazi), out_shape=ja...  21.4 us
    pallas_call x1, Pallas kernels, on_device(): pl.pallas_call(compute_kernel, out_shape=jax.ShapeDtypeStruct(flat.shape,...  5.45 us

profile of v7, /device:TPU:1, one launch (start us, length us, event | category | flops | bytes accessed | tf_op | source)
XLA Modules:
  0.0 26.9 jit_solution(11524847899202375667)
XLA Ops:
  0.0 0.0 copy-start
  0.0 0.0 copy-start.3
  0.0 0.0 copy-start.2
  0.0 0.0 copy-start.1
  0.0 21.4 %shard_map.55.ext_ref = f32[4,20,48,128]{3,2,1,0:T(8,128)S(1)} custom-call(f32[20,16,128]{2,1,0:T(8,128)} %bitcast.8), custom_call_target="tpu_custom_call" | custom-call | tf_op jit(solution)/shard_map/pallas_call | solution.py:181
  21.4 0.0 copy-done
  21.4 0.0 copy-done.3
  21.4 0.0 copy-done.2
  21.4 0.0 copy-done.1
  21.4 5.5 %shard_map.56 = f32[20,16,128]{2,1,0:T(8,128)} custom-call(s32[1,128]{1,0:T(1,128)S(1)} %bitcast.5, f32[1,128]{1,0:T(1,128)S(1)} %bitcast.6, f32[1,128]{1,0:T(1,128)S(1)} %bitcast.7, f32[4,128]{1,0:T(4,128)S(1)} %copy-done, f32[4,20,48,128]{3,2,1,0:T(8,128)S(1)} %shard_map.55.ext_ref), custom_call_target="tpu_custom_call" | custom-call | tf_op jit(solution)/shard_map/pallas_call | solution.py:359
Async XLA Ops:
  0.0 21.4 %copy-start = (f32[4,128]{1,0:T(4,128)S(1)}, f32[4,128]{1,0:T(4,128)}, u32[]{:S(2)}) copy-start(f32[4,128]{1,0:T(4,128)} %stiff_ref.1) | copy-start | bytes 6148
  0.0 21.4 %copy-start.3 = (f32[128]{0:T(128)S(1)}, f32[128]{0:T(128)}, u32[]{:S(2)}) copy-start(f32[128]{0:T(128)} %param.8) | copy-start | bytes 1540
  0.0 21.4 %copy-start.2 = (f32[128]{0:T(128)S(1)}, f32[128]{0:T(128)}, u32[]{:S(2)}) copy-start(f32[128]{0:T(128)} %param.7) | copy-start | bytes 1540
  0.0 21.4 %copy-start.1 = (s32[128]{0:T(128)S(1)}, s32[128]{0:T(128)}, u32[]{:S(2)}) copy-start(s32[128]{0:T(128)} %param.6) | copy-start | bytes 1540

commit v8 on v7

--- a/solution.py
+++ b/solution.py
@@ -13,6 +13,7 @@
 OWN = 16
 LANES = 128
 LEVELS = 4
+PARTS = 4
 time_step = 0.15
 diffuse = 0.05
 
@@ -23,7 +24,7 @@
     has_low, has_high = rad > 0, rad < nrad - 1
 
     has_left, has_right = azi > 0, azi < nazi - 1
-    half = x_ref.shape[0] // 2
+    part = x_ref.shape[0] // PARTS
     everywhere = ((has_left, rad, azi - 1), (has_right, rad, azi + 1), (has_low, rad - 1, azi), (has_high, rad + 1, azi))
 
     barrier = pltpu.get_barrier_semaphore()
@@ -49,7 +50,7 @@
         pl.semaphore_signal(ready, inc=1, device_id=(rad, azi - 1), device_id_type=MESH)
 
     def planes(c):
-        return pl.ds(c * half, half)
+        return pl.ds(c * part, part)
 
     def z_copy(side, t, c, block, src):
         return pltpu.make_async_remote_copy(
@@ -113,16 +114,16 @@
 
     @pl.when(has_left)
     def _():
-        for c in range(2):
+        for c in range(PARTS):
             along(1, 0, c).start()
 
-    for c in range(2):
+    for c in range(PARTS):
         pass_on(azi, c, True)
 
     @pl.when(has_right)
     def _():
         pl.semaphore_wait(ready, 1)
-        for c in range(2):
+        for c in range(PARTS):
             along(0, 0, c).start()
 
     for side, missing in enumerate((has_low, has_high)):
@@ -133,7 +134,7 @@
                 edge(b, side).start()
 
     for t in range(nazi - 1):
-        for c, side in ((0, 0), (0, 1), (1, 0), (1, 1)):
+        for c, side in [(c, side) for c in range(PARTS) for side in range(2)]:
 
             @pl.when(arrives(side, t))
             def _():
@@ -158,20 +159,20 @@
 
             @pl.when(sends(side, t))
             def _():
-                for c in range(2):
+                for c in range(PARTS):
                     along(side, t, c).wait_send()
 
     @pl.when(has_low)
     def _():
         for b in range(nazi):
-            for c in range(2):
+            for c in range(PARTS):
                 radial(0, b, c, False).wait_send()
                 radial(1, b, c, False).wait_recv()
 
     @pl.when(has_high)
     def _():
         for b in range(nazi):
-            for c in range(2):
+            for c in range(PARTS):
                 radial(1, b, c, False).wait_send()
                 radial(0, b, c, False).wait_recv()
 
@@ -186,10 +187,10 @@
         scratch_shapes=[
             pltpu.VMEM((planes, HALO, cells), jnp.float32),
             pltpu.SemaphoreType.DMA,
-            pltpu.SemaphoreType.DMA((2, nazi, 2)),
-            pltpu.SemaphoreType.DMA((2, nazi, 2)),
-            pltpu.SemaphoreType.DMA((2, nazi, 2)),
-            pltpu.SemaphoreType.DMA((2, nazi, 2)),
+            pltpu.SemaphoreType.DMA((2, nazi, PARTS)),
+            pltpu.SemaphoreType.DMA((2, nazi, PARTS)),
+            pltpu.SemaphoreType.DMA((2, nazi, PARTS)),
+            pltpu.SemaphoreType.DMA((2, nazi, PARTS)),
             pltpu.SemaphoreType.DMA((2, nazi)),
             pltpu.SemaphoreType.REGULAR,
         ],
@@ -260,7 +261,7 @@
                 dst[j, plane, s : s + 8, :] = result
         return carry
 
-    lax.fori_loop(0, nazi, body, 0, unroll=4)
+    lax.fori_loop(0, nazi, body, 0, unroll=2)
 
 
 def fill_coefficients(coef, first, shift_ref, spin_ref, drift_ref, stiff_ref):

time: 27 us -> 26 us (0.963)
  Pallas kernels: 26.8 us -> 25.8 us
    pallas_call x1, Pallas kernels: 21.4 us -> 20.2 us  [gathered(): pl.pallas_call(functools.partial(gather_kernel, nrad, nazi), out_shape=ja...]
where the time goes in v8:
time: 26 us; the launch traced here: 25.9 us
  Pallas kernels  25.8 us (99%)
    pallas_call x1, Pallas kernels, gathered(): pl.pallas_call(functools.partial(gather_kernel, nrad, nazi), out_shape=ja...  20.2 us
    pallas_call x1, Pallas kernels, on_device(): pl.pallas_call(compute_kernel, out_shape=jax.ShapeDtypeStruct(flat.shape,...  5.56 us

profile of v8, /device:TPU:1, one launch (start us, length us, event | category | flops | bytes accessed | tf_op | source)
XLA Modules:
  0.0 25.9 jit_solution(68069046817339810)
XLA Ops:
  0.0 0.0 copy-start
  0.0 0.0 copy-start.3
  0.0 0.0 copy-start.2
  0.0 0.0 copy-start.1
  0.0 20.2 %shard_map.55.ext_ref = f32[4,20,48,128]{3,2,1,0:T(8,128)S(1)} custom-call(f32[20,16,128]{2,1,0:T(8,128)} %bitcast.8), custom_call_target="tpu_custom_call" | custom-call | tf_op jit(solution)/shard_map/pallas_call | solution.py:182
  20.3 0.0 copy-done
  20.3 0.0 copy-done.3
  20.3 0.0 copy-done.2
  20.3 0.0 copy-done.1
  20.3 5.6 %shard_map.56 = f32[20,16,128]{2,1,0:T(8,128)} custom-call(s32[1,128]{1,0:T(1,128)S(1)} %bitcast.5, f32[1,128]{1,0:T(1,128)S(1)} %bitcast.6, f32[1,128]{1,0:T(1,128)S(1)} %bitcast.7, f32[4,128]{1,0:T(4,128)S(1)} %copy-done, f32[4,20,48,128]{3,2,1,0:T(8,128)S(1)} %shard_map.55.ext_ref), custom_call_target="tpu_custom_call" | custom-call | tf_op jit(solution)/shard_map/pallas_call | solution.py:360
Async XLA Ops:
  0.0 20.3 %copy-start = (f32[4,128]{1,0:T(4,128)S(1)}, f32[4,128]{1,0:T(4,128)}, u32[]{:S(2)}) copy-start(f32[4,128]{1,0:T(4,128)} %stiff_ref.1) | copy-start | bytes 6148
  0.0 20.3 %copy-start.3 = (f32[128]{0:T(128)S(1)}, f32[128]{0:T(128)}, u32[]{:S(2)}) copy-start(f32[128]{0:T(128)} %param.8) | copy-start | bytes 1540
  0.0 20.3 %copy-start.2 = (f32[128]{0:T(128)S(1)}, f32[128]{0:T(128)}, u32[]{:S(2)}) copy-start(f32[128]{0:T(128)} %param.7) | copy-start | bytes 1540
  0.0 20.3 %copy-start.1 = (s32[128]{0:T(128)S(1)}, s32[128]{0:T(128)}, u32[]{:S(2)}) copy-start(s32[128]{0:T(128)} %param.6) | copy-start | bytes 1540
